TPU v7x, 256 devices: a whole 4x4x8 slice. The times are simulated.
256 devices in a mesh: pipe: 16 (over x, z_hi, core), dp: 16 (over z_lo, y).
Axes of the slice: x: 4, y: 4, z: 8 (z_hi: 2, z_lo: 4; z = z_hi * 4 + z_lo), core: 2. Of those that a mesh axis runs over, the one named last changes fastest.
Arguments:
- stored_inputs: bfloat16 [16, 2, 8192, 512], P('pipe', None, 'dp'), may hold values from -6 to 6
- cotangent: bfloat16 [2, 8192, 512], P(None, 'dp'), may hold values from -0.5 to 0.5
- up_weight: bfloat16 [16, 512, 1024], P('pipe'), may hold values from -0.25 to 0.25
- down_weight: bfloat16 [16, 1024, 512], P('pipe'), may hold values from -0.1875 to 0.1875
- up_buffer: float32 [16, 16, 512, 1024], P('pipe', 'dp'), may hold values from -6 to 6
- down_buffer: float32 [16, 16, 1024, 512], P('pipe', 'dp'), may hold values from -6 to 6
- up_sketch: float32 [16, 1024, 64], P('pipe'), may hold values from -0.1875 to 0.1875
- down_sketch: float32 [16, 512, 64], P('pipe'), may hold values from -0.25 to 0.25
Outputs:
- input_grads: bfloat16 [16, 2, 8192, 512], P('pipe', None, 'dp')
- new_up_buffer: float32 [16, 16, 512, 1024], P('pipe', 'dp')
- new_down_buffer: float32 [16, 16, 1024, 512], P('pipe', 'dp')
- up_update: float32 [16, 512, 1024], P('pipe', 'dp')
- down_update: float32 [16, 1024, 512], P('pipe', 'dp')
All inputs are finite; a program needn't handle non-finite values.
Results may differ from a plain program's by a relative error of at most 0.04.
Values may be sent and summed in bfloat16 or wider, within the bound.
A program may use at most 64 MiB of HBM per device.

v0:
```python
import jax
import jax.numpy as jnp
from jax import lax
from jax.sharding import PartitionSpec as P

inv_root_two = 0.7071067811865476
inv_root_two_pi = 0.3989422804014327


def shifted(value, axis, steps):
    count = lax.axis_size(axis)
    first, last = (max(0, -steps), min(count, count - steps))
    return lax.ppermute(value, axis, [(source, source + steps) for source in range(first, last)])


def gelu_parts(hidden):
    normal_cdf = 0.5 * (1.0 + lax.erf(hidden * inv_root_two))
    density = jnp.exp(-0.5 * hidden * hidden) * inv_root_two_pi
    return (hidden * normal_cdf, normal_cdf + hidden * density)


def contract_last(left, right):
    return lax.dot_general(
        left, right, (((1,), (1,)), ((), ())), preferred_element_type=jnp.float32
    )


def contract_first(left, right):
    return lax.dot_general(
        left, right, (((0,), (0,)), ((), ())), preferred_element_type=jnp.float32
    )


def on_device(
    stored_inputs, cotangent, up_weight, down_weight, up_buffer, down_buffer, up_sketch, down_sketch
):
    high = lax.Precision.HIGHEST
    sections = lax.axis_size("pipe")
    replicas = lax.axis_size("dp")
    position = lax.axis_index("pipe")
    inputs_here = stored_inputs[0]
    micro_count, tok_rows, width = inputs_here.shape
    w_up = up_weight[0]
    w_down = down_weight[0]
    hidden_width = w_up.shape[1]
    pieces = 1
    piece_rows = tok_rows // pieces
    units = micro_count * pieces
    is_last = position == sections - 1

    def backward_unit(dy_bf, inputs_bf, grad_up, grad_down):
        hidden = jnp.dot(inputs_bf, w_up, preferred_element_type=jnp.float32)
        act_val, slope = gelu_parts(hidden)
        act_bf = act_val.astype(jnp.bfloat16)
        d_act = contract_last(dy_bf, w_down)
        dh_bf = (d_act * slope).astype(jnp.bfloat16)
        dx_f = dy_bf.astype(jnp.float32) + contract_last(dh_bf, w_up)
        grad_up = grad_up + contract_first(inputs_bf, dh_bf)
        grad_down = grad_down + contract_first(act_bf, dy_bf)
        return (dx_f.astype(jnp.bfloat16), grad_up, grad_down)

    def tick_step(tick, carry):
        incoming, grad_up, grad_down, collected = carry
        unit_index = tick - (sections - 1 - position)
        active = jnp.logical_and(unit_index >= 0, unit_index < units)
        clipped = jnp.clip(unit_index, 0, units - 1)
        micro_index = clipped // pieces
        row_start = clipped % pieces * piece_rows
        zero_index = jnp.zeros((), jnp.int32)
        inputs_bf = lax.dynamic_slice(
            inputs_here, (micro_index, row_start, zero_index), (1, piece_rows, width)
        )[0]
        cot_bf = lax.dynamic_slice(
            cotangent, (micro_index, row_start, zero_index), (1, piece_rows, width)
        )[0]
        dy_bf = jnp.where(is_last, cot_bf, incoming)

        def run_unit(state):
            grad_up_in, grad_down_in, collected_in = state
            dx_bf, grad_up_out, grad_down_out = backward_unit(
                dy_bf, inputs_bf, grad_up_in, grad_down_in
            )
            collected_out = lax.dynamic_update_slice(
                collected_in, dx_bf[None], (micro_index, row_start, zero_index)
            )
            return (dx_bf, grad_up_out, grad_down_out, collected_out)

        def skip_unit(state):
            return (jnp.zeros_like(incoming),) + tuple(state)

        dx_bf, grad_up, grad_down, collected = lax.cond(
            active, run_unit, skip_unit, (grad_up, grad_down, collected)
        )
        incoming = shifted(dx_bf, "pipe", -1)
        return (incoming, grad_up, grad_down, collected)

    start_carry = (
        jnp.zeros((piece_rows, width), jnp.bfloat16),
        jnp.zeros((width, hidden_width), jnp.float32),
        jnp.zeros((hidden_width, width), jnp.float32),
        jnp.zeros((micro_count, tok_rows, width), jnp.bfloat16),
    )
    final_carry = lax.fori_loop(0, sections + units - 1, tick_step, start_carry)
    grad_up, grad_down, collected = (final_carry[1], final_carry[2], final_carry[3])
    up_sum = grad_up + up_buffer[0, 0]
    down_sum = grad_down + down_buffer[0, 0]
    sketch_up = up_sketch[0]
    sketch_down = down_sketch[0]
    local_up = jnp.dot(up_sum, sketch_up, precision=high)
    local_down = jnp.dot(down_sum, sketch_down, precision=high)
    total_up, total_down = (
        lax.psum(local_up.astype(jnp.bfloat16), "dp").astype(jnp.float32),
        lax.psum(local_down.astype(jnp.bfloat16), "dp").astype(jnp.float32),
    )
    up_upd = lax.dot_general(
        total_up / replicas, sketch_up, (((1,), (1,)), ((), ())), precision=high
    )
    down_upd = lax.dot_general(
        total_down / replicas, sketch_down, (((1,), (1,)), ((), ())), precision=high
    )
    new_up = up_sum - up_upd
    new_down = down_sum - down_upd
    replica_index = lax.axis_index("dp")
    up_rows = width // replicas
    down_rows = hidden_width // replicas
    up_part = lax.dynamic_slice_in_dim(up_upd, replica_index * up_rows, up_rows, 0)
    down_part = lax.dynamic_slice_in_dim(down_upd, replica_index * down_rows, down_rows, 0)
    return (
        collected[None],
        new_up[None, None],
        new_down[None, None],
        up_part[None],
        down_part[None],
    )


def solution(mesh):
    return jax.shard_map(
        on_device,
        mesh=mesh,
        in_specs=(
            P("pipe", None, "dp", None),
            P(None, "dp", None),
            P("pipe", None, None),
            P("pipe", None, None),
            P("pipe", "dp", None, None),
            P("pipe", "dp", None, None),
            P("pipe", None, None),
            P("pipe", None, None),
        ),
        out_specs=(
            P("pipe", None, "dp", None),
            P("pipe", "dp", None, None),
            P("pipe", "dp", None, None),
            P("pipe", "dp", None),
            P("pipe", "dp", None),
        ),
        check_vma=False,
    )
```

profile of v0, /device:TPU:24, one launch (start us, length us, event | category | flops | bytes accessed | tf_op | source)
XLA Modules:
  0.0 531.7 jit_solution(17660812353978190781)
XLA Ops:
  9.1 1.6 broadcast_in_dim.33
  11.0 316.2 %while.21 = (s32[]{:T(128)}, bf16[512,512]{1,0:T(8,128)(2,1)}, f32[512,1024]{1,0:T(8,128)S(1)}, f32[1024,512]{1,0:T(8,128)}, bf16[2,512,512]{2,1,0:T(8,128)(2,1)...) while((s32[]{:T(128)}, bf16[512,512]{1,0:T(8,128)(2,1)}, ...), condition=%wide.region_3.4_spmd, body=%wide.region_0.3_spmd.sunk | while | flops 2694316032 | bytes 61866536 | solution.py:103
  13.1 2.8 collective-permute-done
  18.1 14.7 %collective-permute-done = bf16[512,512]{1,0:T(8,128)(2,1)} collective-permute-done((bf16[512,512]{1,0:T(8,128)(2,1)}, bf16[512,512]{1,0:T(8,128)(2,1)}, u32[]{:S(2)}, u32[]{:S(2)}) %collective-permute-start) | collective-permute-done | bytes 524320 | tf_op jit(solution)/shard_map/while/body/eval_jaxpr/ppermute | solution.py:13
  34.9 13.5 %collective-permute-done = bf16[512,512]{1,0:T(8,128)(2,1)} collective-permute-done((bf16[512,512]{1,0:T(8,128)(2,1)}, bf16[512,512]{1,0:T(8,128)(2,1)}, u32[]{:S(2)}, u32[]{:S(2)}) %collective-permute-start) | collective-permute-done | bytes 524320 | tf_op jit(solution)/shard_map/while/body/eval_jaxpr/ppermute | solution.py:13
  50.5 13.4 %collective-permute-done = bf16[512,512]{1,0:T(8,128)(2,1)} collective-permute-done((bf16[512,512]{1,0:T(8,128)(2,1)}, bf16[512,512]{1,0:T(8,128)(2,1)}, u32[]{:S(2)}, u32[]{:S(2)}) %collective-permute-start) | collective-permute-done | bytes 524320 | tf_op jit(solution)/shard_map/while/body/eval_jaxpr/ppermute | solution.py:13
  66.1 13.4 %collective-permute-done = bf16[512,512]{1,0:T(8,128)(2,1)} collective-permute-done((bf16[512,512]{1,0:T(8,128)(2,1)}, bf16[512,512]{1,0:T(8,128)(2,1)}, u32[]{:S(2)}, u32[]{:S(2)}) %collective-permute-start) | collective-permute-done | bytes 524320 | tf_op jit(solution)/shard_map/while/body/eval_jaxpr/ppermute | solution.py:13
  81.6 16.2 %collective-permute-done = bf16[512,512]{1,0:T(8,128)(2,1)} collective-permute-done((bf16[512,512]{1,0:T(8,128)(2,1)}, bf16[512,512]{1,0:T(8,128)(2,1)}, u32[]{:S(2)}, u32[]{:S(2)}) %collective-permute-start) | collective-permute-done | bytes 524320 | tf_op jit(solution)/shard_map/while/body/eval_jaxpr/ppermute | solution.py:13
  99.9 14.3 %collective-permute-done = bf16[512,512]{1,0:T(8,128)(2,1)} collective-permute-done((bf16[512,512]{1,0:T(8,128)(2,1)}, bf16[512,512]{1,0:T(8,128)(2,1)}, u32[]{:S(2)}, u32[]{:S(2)}) %collective-permute-start) | collective-permute-done | bytes 524320 | tf_op jit(solution)/shard_map/while/body/eval_jaxpr/ppermute | solution.py:13
  116.4 14.3 %collective-permute-done = bf16[512,512]{1,0:T(8,128)(2,1)} collective-permute-done((bf16[512,512]{1,0:T(8,128)(2,1)}, bf16[512,512]{1,0:T(8,128)(2,1)}, u32[]{:S(2)}, u32[]{:S(2)}) %collective-permute-start) | collective-permute-done | bytes 524320 | tf_op jit(solution)/shard_map/while/body/eval_jaxpr/ppermute | solution.py:13
  132.8 14.3 %collective-permute-done = bf16[512,512]{1,0:T(8,128)(2,1)} collective-permute-done((bf16[512,512]{1,0:T(8,128)(2,1)}, bf16[512,512]{1,0:T(8,128)(2,1)}, u32[]{:S(2)}, u32[]{:S(2)}) %collective-permute-start) | collective-permute-done | bytes 524320 | tf_op jit(solution)/shard_map/while/body/eval_jaxpr/ppermute | solution.py:13
  149.3 14.3 %collective-permute-done = bf16[512,512]{1,0:T(8,128)(2,1)} collective-permute-done((bf16[512,512]{1,0:T(8,128)(2,1)}, bf16[512,512]{1,0:T(8,128)(2,1)}, u32[]{:S(2)}, u32[]{:S(2)}) %collective-permute-start) | collective-permute-done | bytes 524320 | tf_op jit(solution)/shard_map/while/body/eval_jaxpr/ppermute | solution.py:13
  165.7 14.3 %collective-permute-done = bf16[512,512]{1,0:T(8,128)(2,1)} collective-permute-done((bf16[512,512]{1,0:T(8,128)(2,1)}, bf16[512,512]{1,0:T(8,128)(2,1)}, u32[]{:S(2)}, u32[]{:S(2)}) %collective-permute-start) | collective-permute-done | bytes 524320 | tf_op jit(solution)/shard_map/while/body/eval_jaxpr/ppermute | solution.py:13
  182.2 14.3 %collective-permute-done = bf16[512,512]{1,0:T(8,128)(2,1)} collective-permute-done((bf16[512,512]{1,0:T(8,128)(2,1)}, bf16[512,512]{1,0:T(8,128)(2,1)}, u32[]{:S(2)}, u32[]{:S(2)}) %collective-permute-start) | collective-permute-done | bytes 524320 | tf_op jit(solution)/shard_map/while/body/eval_jaxpr/ppermute | solution.py:13
  198.6 14.3 %collective-permute-done = bf16[512,512]{1,0:T(8,128)(2,1)} collective-permute-done((bf16[512,512]{1,0:T(8,128)(2,1)}, bf16[512,512]{1,0:T(8,128)(2,1)}, u32[]{:S(2)}, u32[]{:S(2)}) %collective-permute-start) | collective-permute-done | bytes 524320 | tf_op jit(solution)/shard_map/while/body/eval_jaxpr/ppermute | solution.py:13
  215.1 19.2 %collective-permute-done = bf16[512,512]{1,0:T(8,128)(2,1)} collective-permute-done((bf16[512,512]{1,0:T(8,128)(2,1)}, bf16[512,512]{1,0:T(8,128)(2,1)}, u32[]{:S(2)}, u32[]{:S(2)}) %collective-permute-start) | collective-permute-done | bytes 524320 | tf_op jit(solution)/shard_map/while/body/eval_jaxpr/ppermute | solution.py:13
  236.4 49.8 %collective-permute-done = bf16[512,512]{1,0:T(8,128)(2,1)} collective-permute-done((bf16[512,512]{1,0:T(8,128)(2,1)}, bf16[512,512]{1,0:T(8,128)(2,1)}, u32[]{:S(2)}, u32[]{:S(2)}) %collective-permute-start) | collective-permute-done | bytes 524320 | tf_op jit(solution)/shard_map/while/body/eval_jaxpr/ppermute | solution.py:13
  286.2 8.1 %conditional.2 = (bf16[512,512]{1,0:T(8,128)(2,1)}, f32[512,1024]{1,0:T(8,128)S(1)}, f32[1024,512]{1,0:T(8,128)}, bf16[2,512,512]{2,1,0:T(8,128)(2,1)}) conditional(s32[]{:T(128)} %convert_element_type.74, (f32[512,1024]{1,0:T(8,128)S(1)}, f32[1024,512]{1,0:T(8,128)}, bf16[2,512,512]{2,1,0:T(8,128)(2,1)}) %tuple.64, (pred[]{:T(512)}, s32[]{:T(128)}, ...), branch_computations={%region_1.1_spmd, %region_2.2_spmd} | conditional | flops 2694316032 | bytes 59769072 | solution.py:91
  288.9 1.4 fusion.5
  291.7 1.5 bitcast_dynamic-update-slice_fusion
  295.5 16.1 %collective-permute-done = bf16[512,512]{1,0:T(8,128)(2,1)} collective-permute-done((bf16[512,512]{1,0:T(8,128)(2,1)}, bf16[512,512]{1,0:T(8,128)(2,1)}, u32[]{:S(2)}, u32[]{:S(2)}) %collective-permute-start) | collective-permute-done | bytes 524320 | tf_op jit(solution)/shard_map/while/body/eval_jaxpr/ppermute | solution.py:13
  311.7 8.1 %conditional.2 = (bf16[512,512]{1,0:T(8,128)(2,1)}, f32[512,1024]{1,0:T(8,128)S(1)}, f32[1024,512]{1,0:T(8,128)}, bf16[2,512,512]{2,1,0:T(8,128)(2,1)}) conditional(s32[]{:T(128)} %convert_element_type.74, (f32[512,1024]{1,0:T(8,128)S(1)}, f32[1024,512]{1,0:T(8,128)}, bf16[2,512,512]{2,1,0:T(8,128)(2,1)}) %tuple.64, (pred[]{:T(512)}, s32[]{:T(128)}, ...), branch_computations={%region_1.1_spmd, %region_2.2_spmd} | conditional | flops 2694316032 | bytes 59769072 | solution.py:91
  314.4 1.4 fusion.5
  317.2 1.5 bitcast_dynamic-update-slice_fusion
  321.0 6.2 %collective-permute-done = bf16[512,512]{1,0:T(8,128)(2,1)} collective-permute-done((bf16[512,512]{1,0:T(8,128)(2,1)}, bf16[512,512]{1,0:T(8,128)(2,1)}, u32[]{:S(2)}, u32[]{:S(2)}) %collective-permute-start) | collective-permute-done | bytes 524320 | tf_op jit(solution)/shard_map/while/body/eval_jaxpr/ppermute | solution.py:13
  327.2 4.2 convolution_convert_fusion.1
  331.4 2.5 convolution_convert_fusion
  333.9 180.8 %all-reduce.3.cloned.1.call-done = (bf16[512,64]{1,0:T(8,128)(2,1)}, bf16[1024,64]{1,0:T(8,128)(2,1)}) async-done(((bf16[512,64]{1,0:T(8,128)(2,1)}, bf16[1024,64]{1,0:T(8,128)(2,1)}), (bf16[512,64]{1,0:T(8,128)(2,1)}, bf16[1024,64]{1,0:T(8,128)(2,1)})) %all-reduce.3.cloned.1.call-update) | async-done | bytes 196624 | tf_op jit(solution)/shard_map/psum | solution.py:112
  514.7 2.8 fusion.17
  517.6 2.0 subtract_bitcast_fusion.1
  520.3 1.8 fusion.14
  522.1 2.1 subtract_bitcast_fusion
  (104 shorter events, 60.4 us)
Async XLA Ops:
  7.2 320.0 %copy-start = (f32[1,1024,64]{1,2,0:T(8,128)S(1)}, f32[1,1024,64]{1,2,0:T(8,128)}, u32[]{:S(2)}) copy-start(f32[1,1024,64]{1,2,0:T(8,128)} %param.18) | copy-start | bytes 786436
  7.2 507.5 %all-reduce.3.cloned.1.call-start = ((), (), s32[]{:S(2)}) async-start(), calls=%async_computation | async-start | bytes 786432 | tf_op jit(solution)/shard_map/psum | solution.py:112
  9.1 1.8 copy-start.5
  11.8 4.1 collective-permute-start
  16.8 16.0 %collective-permute-start = (bf16[512,512]{1,0:T(8,128)(2,1)}, bf16[512,512]{1,0:T(8,128)(2,1)}, u32[]{:S(2)}, u32[]{:S(2)}) collective-permute-start(bf16[512,512]{1,0:T(8,128)(2,1)} %get-tuple-element.576), channel_id=1, source_target_pairs={{16,0},{32,16},{48,32},{64,48},{80,64},{96,80},{112,96},{128,112},... | collective-permute-start | bytes 1572872 | tf_op jit(solution)/shard_map/while/body/eval_jaxpr/ppermute | solution.py:13
  33.6 14.8 %collective-permute-start = (bf16[512,512]{1,0:T(8,128)(2,1)}, bf16[512,512]{1,0:T(8,128)(2,1)}, u32[]{:S(2)}, u32[]{:S(2)}) collective-permute-start(bf16[512,512]{1,0:T(8,128)(2,1)} %get-tuple-element.576), channel_id=1, source_target_pairs={{16,0},{32,16},{48,32},{64,48},{80,64},{96,80},{112,96},{128,112},... | collective-permute-start | bytes 1572872 | tf_op jit(solution)/shard_map/while/body/eval_jaxpr/ppermute | solution.py:13
  49.2 14.7 %collective-permute-start = (bf16[512,512]{1,0:T(8,128)(2,1)}, bf16[512,512]{1,0:T(8,128)(2,1)}, u32[]{:S(2)}, u32[]{:S(2)}) collective-permute-start(bf16[512,512]{1,0:T(8,128)(2,1)} %get-tuple-element.576), channel_id=1, source_target_pairs={{16,0},{32,16},{48,32},{64,48},{80,64},{96,80},{112,96},{128,112},... | collective-permute-start | bytes 1572872 | tf_op jit(solution)/shard_map/while/body/eval_jaxpr/ppermute | solution.py:13
  64.8 14.7 %collective-permute-start = (bf16[512,512]{1,0:T(8,128)(2,1)}, bf16[512,512]{1,0:T(8,128)(2,1)}, u32[]{:S(2)}, u32[]{:S(2)}) collective-permute-start(bf16[512,512]{1,0:T(8,128)(2,1)} %get-tuple-element.576), channel_id=1, source_target_pairs={{16,0},{32,16},{48,32},{64,48},{80,64},{96,80},{112,96},{128,112},... | collective-permute-start | bytes 1572872 | tf_op jit(solution)/shard_map/while/body/eval_jaxpr/ppermute | solution.py:13
  80.3 17.5 %collective-permute-start = (bf16[512,512]{1,0:T(8,128)(2,1)}, bf16[512,512]{1,0:T(8,128)(2,1)}, u32[]{:S(2)}, u32[]{:S(2)}) collective-permute-start(bf16[512,512]{1,0:T(8,128)(2,1)} %get-tuple-element.576), channel_id=1, source_target_pairs={{16,0},{32,16},{48,32},{64,48},{80,64},{96,80},{112,96},{128,112},... | collective-permute-start | bytes 1572872 | tf_op jit(solution)/shard_map/while/body/eval_jaxpr/ppermute | solution.py:13
  98.7 15.6 %collective-permute-start = (bf16[512,512]{1,0:T(8,128)(2,1)}, bf16[512,512]{1,0:T(8,128)(2,1)}, u32[]{:S(2)}, u32[]{:S(2)}) collective-permute-start(bf16[512,512]{1,0:T(8,128)(2,1)} %get-tuple-element.576), channel_id=1, source_target_pairs={{16,0},{32,16},{48,32},{64,48},{80,64},{96,80},{112,96},{128,112},... | collective-permute-start | bytes 1572872 | tf_op jit(solution)/shard_map/while/body/eval_jaxpr/ppermute | solution.py:13
  115.1 15.6 %collective-permute-start = (bf16[512,512]{1,0:T(8,128)(2,1)}, bf16[512,512]{1,0:T(8,128)(2,1)}, u32[]{:S(2)}, u32[]{:S(2)}) collective-permute-start(bf16[512,512]{1,0:T(8,128)(2,1)} %get-tuple-element.576), channel_id=1, source_target_pairs={{16,0},{32,16},{48,32},{64,48},{80,64},{96,80},{112,96},{128,112},... | collective-permute-start | bytes 1572872 | tf_op jit(solution)/shard_map/while/body/eval_jaxpr/ppermute | solution.py:13
  131.5 15.6 %collective-permute-start = (bf16[512,512]{1,0:T(8,128)(2,1)}, bf16[512,512]{1,0:T(8,128)(2,1)}, u32[]{:S(2)}, u32[]{:S(2)}) collective-permute-start(bf16[512,512]{1,0:T(8,128)(2,1)} %get-tuple-element.576), channel_id=1, source_target_pairs={{16,0},{32,16},{48,32},{64,48},{80,64},{96,80},{112,96},{128,112},... | collective-permute-start | bytes 1572872 | tf_op jit(solution)/shard_map/while/body/eval_jaxpr/ppermute | solution.py:13
  148.0 15.6 %collective-permute-start = (bf16[512,512]{1,0:T(8,128)(2,1)}, bf16[512,512]{1,0:T(8,128)(2,1)}, u32[]{:S(2)}, u32[]{:S(2)}) collective-permute-start(bf16[512,512]{1,0:T(8,128)(2,1)} %get-tuple-element.576), channel_id=1, source_target_pairs={{16,0},{32,16},{48,32},{64,48},{80,64},{96,80},{112,96},{128,112},... | collective-permute-start | bytes 1572872 | tf_op jit(solution)/shard_map/while/body/eval_jaxpr/ppermute | solution.py:13
  164.4 15.6 %collective-permute-start = (bf16[512,512]{1,0:T(8,128)(2,1)}, bf16[512,512]{1,0:T(8,128)(2,1)}, u32[]{:S(2)}, u32[]{:S(2)}) collective-permute-start(bf16[512,512]{1,0:T(8,128)(2,1)} %get-tuple-element.576), channel_id=1, source_target_pairs={{16,0},{32,16},{48,32},{64,48},{80,64},{96,80},{112,96},{128,112},... | collective-permute-start | bytes 1572872 | tf_op jit(solution)/shard_map/while/body/eval_jaxpr/ppermute | solution.py:13
  180.9 15.6 %collective-permute-start = (bf16[512,512]{1,0:T(8,128)(2,1)}, bf16[512,512]{1,0:T(8,128)(2,1)}, u32[]{:S(2)}, u32[]{:S(2)}) collective-permute-start(bf16[512,512]{1,0:T(8,128)(2,1)} %get-tuple-element.576), channel_id=1, source_target_pairs={{16,0},{32,16},{48,32},{64,48},{80,64},{96,80},{112,96},{128,112},... | collective-permute-start | bytes 1572872 | tf_op jit(solution)/shard_map/while/body/eval_jaxpr/ppermute | solution.py:13
  197.3 15.6 %collective-permute-start = (bf16[512,512]{1,0:T(8,128)(2,1)}, bf16[512,512]{1,0:T(8,128)(2,1)}, u32[]{:S(2)}, u32[]{:S(2)}) collective-permute-start(bf16[512,512]{1,0:T(8,128)(2,1)} %get-tuple-element.576), channel_id=1, source_target_pairs={{16,0},{32,16},{48,32},{64,48},{80,64},{96,80},{112,96},{128,112},... | collective-permute-start | bytes 1572872 | tf_op jit(solution)/shard_map/while/body/eval_jaxpr/ppermute | solution.py:13
  213.8 20.5 %collective-permute-start = (bf16[512,512]{1,0:T(8,128)(2,1)}, bf16[512,512]{1,0:T(8,128)(2,1)}, u32[]{:S(2)}, u32[]{:S(2)}) collective-permute-start(bf16[512,512]{1,0:T(8,128)(2,1)} %get-tuple-element.576), channel_id=1, source_target_pairs={{16,0},{32,16},{48,32},{64,48},{80,64},{96,80},{112,96},{128,112},... | collective-permute-start | bytes 1572872 | tf_op jit(solution)/shard_map/while/body/eval_jaxpr/ppermute | solution.py:13
  235.1 51.1 %collective-permute-start = (bf16[512,512]{1,0:T(8,128)(2,1)}, bf16[512,512]{1,0:T(8,128)(2,1)}, u32[]{:S(2)}, u32[]{:S(2)}) collective-permute-start(bf16[512,512]{1,0:T(8,128)(2,1)} %get-tuple-element.576), channel_id=1, source_target_pairs={{16,0},{32,16},{48,32},{64,48},{80,64},{96,80},{112,96},{128,112},... | collective-permute-start | bytes 1572872 | tf_op jit(solution)/shard_map/while/body/eval_jaxpr/ppermute | solution.py:13
  286.2 1.5 copy-start.6
  288.9 1.6 copy-start.1
  291.7 2.4 copy-start.2
  294.2 17.4 %collective-permute-start = (bf16[512,512]{1,0:T(8,128)(2,1)}, bf16[512,512]{1,0:T(8,128)(2,1)}, u32[]{:S(2)}, u32[]{:S(2)}) collective-permute-start(bf16[512,512]{1,0:T(8,128)(2,1)} %get-tuple-element.576), channel_id=1, source_target_pairs={{16,0},{32,16},{48,32},{64,48},{80,64},{96,80},{112,96},{128,112},... | collective-permute-start | bytes 1572872 | tf_op jit(solution)/shard_map/while/body/eval_jaxpr/ppermute | solution.py:13
  314.4 1.6 copy-start.1
  317.2 2.3 copy-start.2
  319.8 7.4 %collective-permute-start = (bf16[512,512]{1,0:T(8,128)(2,1)}, bf16[512,512]{1,0:T(8,128)(2,1)}, u32[]{:S(2)}, u32[]{:S(2)}) collective-permute-start(bf16[512,512]{1,0:T(8,128)(2,1)} %get-tuple-element.576), channel_id=1, source_target_pairs={{16,0},{32,16},{48,32},{64,48},{80,64},{96,80},{112,96},{128,112},... | collective-permute-start | bytes 1572872 | tf_op jit(solution)/shard_map/while/body/eval_jaxpr/ppermute | solution.py:13
  327.2 4.2 copy-start.3
  327.2 4.2 copy-start.8
  327.2 4.2 copy-start.12
  514.7 2.8 copy-start.7
  517.6 2.7 copy-start.13
  517.6 4.5 copy-start.9
  519.6 2.5 copy-start.4
  (7 other events, 8.4 us)
Sparse Core Ops, SparseCore 0:
  334.0 180.6 all-reduce.2
where the time goes:
time: 537 us; the launch traced here: 532 us
  waiting for transfers between devices  446 us (83%)
  starting transfers between devices  21.8 us (4%)
  matrix products  21.7 us (4%)
  local copies, waits for them, and re-layouts  20.5 us (4%)
  between operations  14.1 us (3%)
  other arithmetic  6.77 us (1%)
    ppermute x17, waiting for transfers between devices, shifted(): lax.ppermute(value, axis, [(source, source + steps) for source in range(f...  266 us
    psum x1, waiting for transfers between devices, on_device(): lax.psum(local_up.astype(jnp.bfloat16), 'dp').astype(jnp.float32)  181 us
    ppermute x17, starting transfers between devices, shifted(): lax.ppermute(value, axis, [(source, source + steps) for source in range(f...  21.8 us
    another operation x16, local copies, waits for them, and re-layouts  13.3 us
  transfers between devices with their start and end apart: 18, of which 18 were waited for; matrix products, arithmetic and copies ran while one was open for 0% of the time, Pallas kernels for 0%

commit v1 on v0

v1 whole, which is shorter than its diff:
```python
import jax
import jax.numpy as jnp
from jax import lax
from jax.experimental import pallas as pl
from jax.experimental.pallas import tpu as pltpu
from jax.sharding import PartitionSpec as P

MESH = pl.DeviceIdType.MESH
BF = jnp.bfloat16
F32 = jnp.float32
SECTIONS = 16
REPLICAS = 16
D = 512
FF = 1024
RANK = 64
ROWS = 1024
PIECE = 64
BATCH = 256
PIECES = ROWS // PIECE
PER_BATCH = BATCH // PIECE
BATCHES = ROWS // BATCH
PACKED = (D + FF) // 2
BLOCK = PACKED // REPLICAS
inv_root_two = 0.7071067811865476
inv_root_two_pi = 0.3989422804014327


def matmul(left, right):
    return jnp.dot(left, right, preferred_element_type=F32)


def contract_first(left, right):
    return lax.dot_general(left, right, (((0,), (0,)), ((), ())), preferred_element_type=F32)


def contract_last(left, right):
    return lax.dot_general(left, right, (((1,), (1,)), ((), ())), preferred_element_type=F32)


def remote(src, dst, send_sem, recv_sem, device):
    return pltpu.make_async_remote_copy(
        src_ref=src,
        dst_ref=dst,
        send_sem=send_sem,
        recv_sem=recv_sem,
        device_id=device,
        device_id_type=MESH,
    )


def relay_kernel(
    x_hbm, cot_hbm, wu_hbm, wd_hbm, ub_hbm, db_hbm, us_hbm, ds_hbm,
    dx_hbm, usum_hbm, dsum_hbm, tot_up, tot_down,
    x, dy, dx, dh, act, slope, wu, wd, wut, wdt, gu, gd, su, sd, ssu, ssd,
    z, zbf, rs, ag,
    load_sem, out_sem, sum_sem, hop_send, hop_recv, rs_send, rs_recv, ag_send, ag_recv,
):
    pos = lax.axis_index("pipe")
    me = lax.axis_index("dp")
    first = pos == SECTIONS - 1
    last = pos == 0
    prev = jnp.maximum(pos - 1, 0)
    following = jnp.minimum(pos + 1, SECTIONS - 1)

    loads = [
        pltpu.make_async_copy(src, dst, load_sem.at[k])
        for k, (src, dst) in enumerate(
            [(wu_hbm, wu), (x_hbm, x), (wd_hbm, wd), (us_hbm, su), (ds_hbm, sd), (ub_hbm, gu), (db_hbm, gd)]
        )
    ]
    cot_load = pltpu.make_async_copy(cot_hbm, dy, load_sem.at[7])
    loads[0].start()
    loads[1].start()
    loads[2].start()

    @pl.when(first)
    def _():
        cot_load.start()

    for copy in loads[3:]:
        copy.start()

    barrier = pltpu.get_barrier_semaphore()

    def greet(step, carry):
        peer = lax.rem(me + step, REPLICAS)
        pl.semaphore_signal(barrier, inc=1, device_id=(pos, peer), device_id_type=MESH)
        return carry

    @pl.when(jnp.logical_not(last))
    def _():
        pl.semaphore_signal(barrier, inc=1, device_id=(prev, me), device_id_type=MESH)

    @pl.when(jnp.logical_not(first))
    def _():
        pl.semaphore_signal(barrier, inc=1, device_id=(following, me), device_id_type=MESH)

    lax.fori_loop(1, REPLICAS, greet, 0)

    def piece_rows(index):
        return pl.ds(pl.multiple_of(index * PIECE, PIECE), PIECE)

    def batch_rows(index):
        return pl.ds(pl.multiple_of(index * BATCH, BATCH), BATCH)

    def forward(rows):
        hidden = matmul(x[rows, :], wu[...])
        cdf = 0.5 * (1.0 + lax.erf(hidden * inv_root_two))
        density = jnp.exp(-0.5 * hidden * hidden) * inv_root_two_pi
        act[rows, :] = (hidden * cdf).astype(BF)
        slope[rows, :] = cdf + hidden * density

    def hop(index, target):
        rows = piece_rows(index)
        return remote(
            dx.at[rows, :], dy.at[rows, :], hop_send.at[index], hop_recv.at[index], (target, me)
        )

    def grads_out(index):
        rows = piece_rows(index)
        return pltpu.make_async_copy(dx.at[rows, :], dx_hbm.at[rows, :], out_sem.at[index])

    loads[0].wait()
    loads[1].wait()
    loads[2].wait()
    wdt[...] = wd[...].T
    wut[...] = wu[...].T

    def buffer_sketch():
        loads[3].wait()
        loads[4].wait()
        loads[5].wait()
        loads[6].wait()
        up = su[...].astype(BF)
        zero_up = jnp.zeros_like(up)
        ssu[...] = jnp.concatenate([up, zero_up, zero_up, up], axis=1)
        down = sd[...].astype(BF)
        zero_down = jnp.zeros_like(down)
        ssd[...] = jnp.concatenate([down, zero_down, zero_down, down], axis=1)
        z[0 : D // 2, :] = matmul(gu[0 : D // 2, :].astype(BF), ssu[:, 0:128]) + matmul(
            gu[D // 2 : D, :].astype(BF), ssu[:, 128:256]
        )
        z[D // 2 : PACKED, :] = matmul(gd[0 : FF // 2, :].astype(BF), ssd[:, 0:128]) + matmul(
            gd[FF // 2 : FF, :].astype(BF), ssd[:, 128:256]
        )

    @pl.when(jnp.logical_not(first))
    def _():
        def forward_batch(index, carry):
            forward(piece_rows(index))
            return carry

        lax.fori_loop(0, PIECES, forward_batch, 0)
        buffer_sketch()

    pl.semaphore_wait(
        barrier, REPLICAS - 1 + jnp.where(first, 0, 1) + jnp.where(last, 0, 1)
    )

    @pl.when(first)
    def _():
        cot_load.wait()

    def run_piece(index):
        rows = piece_rows(index)

        @pl.when(first)
        def _():
            forward(rows)

        @pl.when(jnp.logical_not(first))
        def _():
            hop(index, prev).wait_recv()

        dy_piece = dy[rows, :]
        dh_piece = (matmul(dy_piece, wdt[...]) * slope[rows, :]).astype(BF)
        dx[rows, :] = (dy_piece.astype(F32) + matmul(dh_piece, wut[...])).astype(BF)

        @pl.when(jnp.logical_not(last))
        def _():
            hop(index, prev).start()

        dh[rows, :] = dh_piece
        grads_out(index).start()

    def sketch(index):
        rows = batch_rows(index)
        up = matmul(dh[rows, :], ssu[...]).astype(BF)
        down = matmul(dy[rows, :], ssd[...]).astype(BF)
        z[0 : D // 2, :] += contract_first(x[rows, 0 : D // 2], up[:, 0:128]) + contract_first(
            x[rows, D // 2 : D], up[:, 128:256]
        )
        z[D // 2 : PACKED, :] += contract_first(act[rows, 0 : FF // 2], down[:, 0:128]) + contract_first(
            act[rows, FF // 2 : FF], down[:, 128:256]
        )

    def weight_grads(index):
        rows = batch_rows(index)
        gu[...] += contract_first(x[rows, :], dh[rows, :])
        gd[...] += contract_first(act[rows, :], dy[rows, :])

    def run_batch(batch, carry):
        def inner(piece, inner_carry):
            run_piece(batch * PER_BATCH + piece)
            return inner_carry

        lax.fori_loop(0, PER_BATCH, inner, 0)

        @pl.when(jnp.logical_and(first, batch == 0))
        def _():
            buffer_sketch()

        sketch(batch)

        @pl.when(batch < BATCHES - 1)
        def _():
            weight_grads(batch)

        return carry

    lax.fori_loop(0, BATCHES, run_batch, 0)

    def block_rows(index):
        return pl.ds(pl.multiple_of(index * BLOCK, BLOCK), BLOCK)

    zbf[...] = z[...].astype(BF)

    def scatter(step):
        peer = lax.rem(me + step, REPLICAS)
        return remote(zbf.at[block_rows(peer), :], rs.at[me], rs_send.at[step], rs_recv.at[me], (pos, peer))

    def gather(step):
        peer = lax.rem(me + step, REPLICAS)
        mine = block_rows(me)
        return remote(ag.at[mine, :], ag.at[mine, :], ag_send.at[step], ag_recv.at[me], (pos, peer))

    def scatter_start(step, carry):
        scatter(step).start()
        return carry

    def scatter_wait(step, carry):
        source = lax.rem(me + step, REPLICAS)
        remote(zbf.at[block_rows(me), :], rs.at[source], rs_send.at[step], rs_recv.at[source], (pos, source)).wait_recv()
        return carry + rs[source].astype(F32)

    def gather_start(step, carry):
        gather(step).start()
        return carry

    def gather_wait(step, carry):
        source = lax.rem(me + step, REPLICAS)
        theirs = block_rows(source)
        remote(ag.at[theirs, :], ag.at[theirs, :], ag_send.at[step], ag_recv.at[source], (pos, source)).wait_recv()
        return carry

    def sends_done(step, carry):
        scatter(step).wait_send()
        gather(step).wait_send()
        return carry

    lax.fori_loop(1, REPLICAS, scatter_start, 0)
    weight_grads(BATCHES - 1)
    sums_out = [
        pltpu.make_async_copy(gu, usum_hbm, sum_sem.at[0]),
        pltpu.make_async_copy(gd, dsum_hbm, sum_sem.at[1]),
    ]
    for copy in sums_out:
        copy.start()
    total = lax.fori_loop(1, REPLICAS, scatter_wait, z[block_rows(me), :])
    ag[block_rows(me), :] = total.astype(BF)
    lax.fori_loop(1, REPLICAS, gather_start, 0)

    def pieces_done(index, carry):
        grads_out(index).wait()

        @pl.when(jnp.logical_not(last))
        def _():
            hop(index, prev).wait_send()

        return carry

    lax.fori_loop(0, PIECES, pieces_done, 0)
    lax.fori_loop(1, REPLICAS, gather_wait, 0)
    tot_up[0 : D // 2, :] = ag[0 : D // 2, 0:RANK]
    tot_up[D // 2 : D, :] = ag[0 : D // 2, RANK : 2 * RANK]
    tot_down[0 : FF // 2, :] = ag[D // 2 : PACKED, 0:RANK]
    tot_down[FF // 2 : FF, :] = ag[D // 2 : PACKED, RANK : 2 * RANK]
    lax.fori_loop(1, REPLICAS, sends_done, 0)
    for copy in sums_out:
        copy.wait()


STEPS = 4


def update_kernel(
    tot_up, tot_down, su, sd, usum, dsum, dx_in, new_up, new_down, up_part, down_part, dx_out, ssu, ssd, sem
):
    step = pl.program_id(0)
    me = lax.axis_index("dp")
    copy = pltpu.make_async_copy(dx_in, dx_out, sem)

    @pl.when(step == 0)
    def _():
        copy.start()
        ssu[...] = (su[...] * (1.0 / REPLICAS)).astype(BF)
        ssd[...] = (sd[...] * (1.0 / REPLICAS)).astype(BF)
        up_rows = D // REPLICAS
        down_rows = FF // REPLICAS
        up_part[...] = contract_last(tot_up[pl.ds(pl.multiple_of(me * up_rows, up_rows), up_rows), :], ssu[...])
        down_part[...] = contract_last(
            tot_down[pl.ds(pl.multiple_of(me * down_rows, down_rows), down_rows), :], ssd[...]
        )

    ub = D // STEPS
    db = FF // STEPS
    new_up[...] = usum[...] - contract_last(tot_up[pl.ds(pl.multiple_of(step * ub, ub), ub), :], ssu[...])
    new_down[...] = dsum[...] - contract_last(tot_down[pl.ds(pl.multiple_of(step * db, db), db), :], ssd[...])

    @pl.when(step == STEPS - 1)
    def _():
        copy.wait()


def on_device(
    stored_inputs, cotangent, up_weight, down_weight, up_buffer, down_buffer, up_sketch, down_sketch
):
    any_spec = pl.BlockSpec(memory_space=pl.ANY)
    vmem = pl.BlockSpec(memory_space=pltpu.VMEM)
    x = stored_inputs.reshape(ROWS, D)
    cot = cotangent.reshape(ROWS, D)
    dx, usum, dsum, tot_up, tot_down = pl.pallas_call(
        relay_kernel,
        name="relay",
        out_shape=(
            jax.ShapeDtypeStruct((ROWS, D), BF),
            jax.ShapeDtypeStruct((D, FF), F32),
            jax.ShapeDtypeStruct((FF, D), F32),
            jax.ShapeDtypeStruct((D, RANK), BF),
            jax.ShapeDtypeStruct((FF, RANK), BF),
        ),
        in_specs=[any_spec] * 8,
        out_specs=(any_spec, any_spec, any_spec, vmem, vmem),
        scratch_shapes=[
            pltpu.VMEM((ROWS, D), BF),
            pltpu.VMEM((ROWS, D), BF),
            pltpu.VMEM((ROWS, D), BF),
            pltpu.VMEM((ROWS, FF), BF),
            pltpu.VMEM((ROWS, FF), BF),
            pltpu.VMEM((ROWS, FF), F32),
            pltpu.VMEM((D, FF), BF),
            pltpu.VMEM((FF, D), BF),
            pltpu.VMEM((FF, D), BF),
            pltpu.VMEM((D, FF), BF),
            pltpu.VMEM((D, FF), F32),
            pltpu.VMEM((FF, D), F32),
            pltpu.VMEM((FF, RANK), F32),
            pltpu.VMEM((D, RANK), F32),
            pltpu.VMEM((FF, 4 * RANK), BF),
            pltpu.VMEM((D, 4 * RANK), BF),
            pltpu.VMEM((PACKED, 2 * RANK), F32),
            pltpu.VMEM((PACKED, 2 * RANK), BF),
            pltpu.VMEM((REPLICAS, BLOCK, 2 * RANK), BF),
            pltpu.VMEM((PACKED, 2 * RANK), BF),
            pltpu.SemaphoreType.DMA((8,)),
            pltpu.SemaphoreType.DMA((PIECES,)),
            pltpu.SemaphoreType.DMA((2,)),
            pltpu.SemaphoreType.DMA((PIECES,)),
            pltpu.SemaphoreType.DMA((PIECES,)),
            pltpu.SemaphoreType.DMA((REPLICAS,)),
            pltpu.SemaphoreType.DMA((REPLICAS,)),
            pltpu.SemaphoreType.DMA((REPLICAS,)),
            pltpu.SemaphoreType.DMA((REPLICAS,)),
        ],
        compiler_params=pltpu.CompilerParams(
            collective_id=0, has_side_effects=True, vmem_limit_bytes=48 * 2**20
        ),
    )(
        x, cot, up_weight[0], down_weight[0], up_buffer[0, 0], down_buffer[0, 0], up_sketch[0], down_sketch[0]
    )
    full_up = pl.BlockSpec((D, RANK), lambda i: (0, 0))
    full_down = pl.BlockSpec((FF, RANK), lambda i: (0, 0))
    block_up = pl.BlockSpec((D // STEPS, FF), lambda i: (i, 0))
    block_down = pl.BlockSpec((FF // STEPS, D), lambda i: (i, 0))
    new_up, new_down, up_part, down_part, grads = pl.pallas_call(
        update_kernel,
        name="update",
        grid=(STEPS,),
        out_shape=(
            jax.ShapeDtypeStruct((D, FF), F32),
            jax.ShapeDtypeStruct((FF, D), F32),
            jax.ShapeDtypeStruct((D // REPLICAS, FF), F32),
            jax.ShapeDtypeStruct((FF // REPLICAS, D), F32),
            jax.ShapeDtypeStruct((ROWS, D), BF),
        ),
        in_specs=[
            full_up,
            full_down,
            full_down,
            full_up,
            block_up,
            block_down,
            any_spec,
        ],
        out_specs=(
            block_up,
            block_down,
            pl.BlockSpec((D // REPLICAS, FF), lambda i: (0, 0)),
            pl.BlockSpec((FF // REPLICAS, D), lambda i: (0, 0)),
            any_spec,
        ),
        scratch_shapes=[
            pltpu.VMEM((FF, RANK), BF),
            pltpu.VMEM((D, RANK), BF),
            pltpu.SemaphoreType.DMA,
        ],
        compiler_params=pltpu.CompilerParams(vmem_limit_bytes=32 * 2**20),
    )(tot_up, tot_down, up_sketch[0], down_sketch[0], usum, dsum, dx)
    return (
        grads.reshape(1, 2, ROWS // 2, D),
        new_up[None, None],
        new_down[None, None],
        up_part[None],
        down_part[None],
    )


def solution(mesh):
    return jax.shard_map(
        on_device,
        mesh=mesh,
        in_specs=(
            P("pipe", None, "dp", None),
            P(None, "dp", None),
            P("pipe", None, None),
            P("pipe", None, None),
            P("pipe", "dp", None, None),
            P("pipe", "dp", None, None),
            P("pipe", None, None),
            P("pipe", None, None),
        ),
        out_specs=(
            P("pipe", None, "dp", None),
            P("pipe", "dp", None, None),
            P("pipe", "dp", None, None),
            P("pipe", "dp", None),
            P("pipe", "dp", None),
        ),
        check_vma=False,
    )
```

time: 537 us -> 126 us (0.23)
  waiting for transfers between devices: 446 us -> 0 us
  Pallas kernels: 0 us -> 114 us
  starting transfers between devices: 21.8 us -> 0 us
  matrix products: 21.7 us -> 0 us
  between operations: 14.1 us -> 0.67 us
  local copies, waits for them, and re-layouts: 20.5 us -> 9.02 us
  other arithmetic: 6.77 us -> 0 us
    ppermute x17 -> x0, waiting for transfers between devices: 266 us -> none  [shifted(): lax.ppermute(value, axis, [(source, source + steps) for source in range(f...]
    psum x1 -> x0, waiting for transfers between devices: 181 us -> none  [on_device(): lax.psum(local_up.astype(jnp.bfloat16), 'dp').astype(jnp.float32)]
    pallas_call x0 -> x2, Pallas kernels: none -> 114 us  [the longest x1 111 us: on_device(): pl.pallas_call(relay_kernel, name='relay', out_shape=(jax.ShapeDtypeStruc...]
    ppermute x17 -> x0, starting transfers between devices: 21.8 us -> none  [shifted(): lax.ppermute(value, axis, [(source, source + steps) for source in range(f...]
    dot_general x14 -> x0, matrix products: 21.7 us -> none  [the longest x4 5.86 us: contract_last(): lax.dot_general(left, right, (((1,), (1,)), ((), ())), preferred_element_...]
    another operation x16 -> x0, local copies, waits for them, and re-layouts: 13.3 us -> none
    unnamed x18 -> x12, local copies, waits for them, and re-layouts: 0.04 us -> 9.02 us
  transfers between devices with their start and end apart: 18 -> 0, of which waited for: 18 -> 0; matrix products, arithmetic and copies ran while one was open for 0% -> 0% of each run, Pallas kernels for 0% -> 0%
where the time goes in v1:
time: 126 us; the launch traced here: 124 us
  Pallas kernels  114 us (90%)
  local copies, waits for them, and re-layouts  9.02 us (7%)
    pallas_call x1, Pallas kernels, on_device(): pl.pallas_call(relay_kernel, name='relay', out_shape=(jax.ShapeDtypeStruc...  111 us
    unnamed x12, local copies, waits for them, and re-layouts  9.02 us
    pallas_call x1, Pallas kernels, on_device(): pl.pallas_call(update_kernel, name='update', grid=(STEPS,), out_shape=(ja...  3.23 us

profile of v1, /device:TPU:24, one launch (start us, length us, event | category | flops | bytes accessed | tf_op | source)
XLA Modules:
  0.0 124.1 jit_solution(17837512527719675884)
XLA Ops:
  0.6 1.0 copy.14
  1.7 1.1 copy.13
  2.8 0.0 copy-start.2
  2.8 1.2 copy-done.2
  4.1 0.0 copy-start.3
  4.1 1.2 copy-done.3
  5.3 0.0 copy-start.4
  5.3 1.2 copy-done.4
  6.5 111.1 %relay.1 = (bf16[1024,512]{1,0:T(8,128)(2,1)S(1)}, f32[512,1024]{1,0:T(8,128)}, f32[1024,512]{1,0:T(8,128)}, bf16[512,64]{1,0:T(8,128)(2,1)S(1)}, bf16[1024,64]{1,0:T(8,128)(2,1)S(1)}) custom-call(bf16[1024,512]{1,0:T(8,128)(2,1)S(1)} %bitcast.17, bf16[1024,512]{1,0:T(8,128)(2,1)S(1)} %bitcast.18, bf16[512,1024]{1,0:T(8,128)(2,1)S(1)} %bitcast.19, ...), custom_call_target="tpu_custom_call" | custom-call | tf_op jit(solution)/shard_map/relay/pallas_call | solution.py:332
  117.6 0.0 copy-start
  117.7 1.6 %copy-done = f32[512,1024]{1,0:T(8,128)S(1)} copy-done((f32[512,1024]{1,0:T(8,128)S(1)}, f32[512,1024]{1,0:T(8,128)}, u32[]{:S(2)}) %copy-start) | copy-done | bytes 2097176
  119.2 0.0 copy-start.1
  119.2 1.6 %copy-done.1 = f32[1024,512]{1,0:T(8,128)S(1)} copy-done((f32[1024,512]{1,0:T(8,128)S(1)}, f32[1024,512]{1,0:T(8,128)}, u32[]{:S(2)}) %copy-start.1) | copy-done | bytes 2097176
  120.8 3.2 %update.1 = (f32[512,1024]{1,0:T(8,128)}, f32[1024,512]{1,0:T(8,128)}, f32[32,1024]{1,0:T(8,128)}, f32[64,512]{1,0:T(8,128)}, bf16[1024,512]{1,0:T(8,128)(2,1)}) custom-call(bf16[512,64]{1,0:T(8,128)(2,1)S(1)} %get-tuple-element.15.tot_up, bf16[1024,64]{1,0:T(8,128)(2,1)S(1)} %get-tuple-element.16.tot_down, f32[1024,64]{1,0:T(8,128)S(1)} %bitcast.14, ...), custom_call_target="tpu_custom_call" | custom-call | tf_op jit(solution)/shard_map/update/pallas_call | solution.py:385
Async XLA Ops:
  2.8 1.2 copy-start.2
  4.1 1.2 copy-start.3
  5.3 1.2 copy-start.4
  117.6 1.6 %copy-start = (f32[512,1024]{1,0:T(8,128)S(1)}, f32[512,1024]{1,0:T(8,128)}, u32[]{:S(2)}) copy-start(f32[512,1024]{1,0:T(8,128)} %get-tuple-element.17.usum) | copy-start | bytes 6291460
  119.2 1.6 %copy-start.1 = (f32[1024,512]{1,0:T(8,128)S(1)}, f32[1024,512]{1,0:T(8,128)}, u32[]{:S(2)}) copy-start(f32[1024,512]{1,0:T(8,128)} %get-tuple-element.18.dsum) | copy-start | bytes 6291460

commit v2 on v1

v2 whole, which is shorter than its diff:
```python
import jax
import jax.numpy as jnp
from jax import lax
from jax.experimental import pallas as pl
from jax.experimental.pallas import tpu as pltpu
from jax.sharding import PartitionSpec as P

MESH = pl.DeviceIdType.MESH
BF = jnp.bfloat16
F32 = jnp.float32
SECTIONS = 16
REPLICAS = 16
D = 512
FF = 1024
RANK = 64
ROWS = 1024
CHIPS = SECTIONS // 2
PIECE = 64
GROUP = 128
PIECES = ROWS // PIECE
GROUPS = ROWS // GROUP
PER_GROUP = GROUP // PIECE
PACKED = (D + FF) // 2
BLOCK = PACKED // REPLICAS
inv_root_two = 0.7071067811865476
inv_root_two_pi = 0.3989422804014327


def matmul(left, right):
    return jnp.dot(left, right, preferred_element_type=F32)


def contract_first(left, right):
    return lax.dot_general(left, right, (((0,), (0,)), ((), ())), preferred_element_type=F32)


def remote(src, dst, send_sem, recv_sem, device):
    return pltpu.make_async_remote_copy(
        src_ref=src,
        dst_ref=dst,
        send_sem=send_sem,
        recv_sem=recv_sem,
        device_id=device,
        device_id_type=MESH,
    )


def relay_kernel(
    x_hbm, cot_hbm, wu_hbm, wd_hbm, ub_hbm, db_hbm, us_hbm, ds_hbm,
    dx_hbm, usum_hbm, dsum_hbm, tot_up, tot_down,
    x, dy, dh, act, gu, gd, slope, wu, wd, wut, wdt, su, sd, ssu, ssd,
    z, zbf, rs, ag,
    load_sem, out_sem, give_send, give_recv, hop_send, hop_recv,
    side_send, side_recv, rs_send, rs_recv, ag_send, ag_recv,
):
    pos = lax.axis_index("pipe")
    me = lax.axis_index("dp")
    core = lax.rem(pos, 2)
    chip = pos // 2
    first = chip == CHIPS - 1
    last = chip == 0
    ends = jnp.logical_or(first, last)
    mid = jnp.logical_not(ends)
    upper = core == 1
    lower = core == 0
    home = 1 - core
    sends_hop = jnp.logical_or(jnp.logical_and(first, lower), jnp.logical_and(mid, upper))
    takes_hop = jnp.logical_and(upper, jnp.logical_not(first))
    gives_now = jnp.logical_and(mid, lower)
    takes_now = jnp.logical_and(mid, upper)
    late = jnp.logical_or(first, takes_now)
    partner = 2 * chip + 1 - core
    target = 2 * jnp.maximum(chip - 1, 0) + 1
    ahead = jnp.minimum(chip + 1, CHIPS - 1)
    source = 2 * ahead + jnp.where(ahead == CHIPS - 1, 0, 1)

    loads = [
        pltpu.make_async_copy(src, dst, load_sem.at[k])
        for k, (src, dst) in enumerate(
            [
                (wu_hbm, wu.at[home]),
                (x_hbm, x.at[home]),
                (wd_hbm, wd.at[home]),
                (us_hbm, su),
                (ds_hbm, sd),
                (ub_hbm, gu),
                (db_hbm, gd),
            ]
        )
    ]
    cot_load = pltpu.make_async_copy(cot_hbm, dy.at[0], load_sem.at[7])
    takes_cot = jnp.logical_and(first, upper)
    gives = [
        remote(src, dst, give_send.at[k], give_recv.at[k], (partner, me))
        for k, (src, dst) in enumerate([(wu_hbm, wu.at[1]), (x_hbm, x.at[1]), (wd_hbm, wd.at[1])])
    ]
    for copy in loads[:3]:
        copy.start()

    @pl.when(takes_cot)
    def _():
        cot_load.start()

    for copy in loads[3:]:
        copy.start()

    barrier = pltpu.get_barrier_semaphore()

    def greet(step, carry):
        peer = lax.rem(me + step, REPLICAS)
        pl.semaphore_signal(barrier, inc=1, device_id=(pos, peer), device_id_type=MESH)
        return carry

    pl.semaphore_signal(barrier, inc=1, device_id=(partner, me), device_id_type=MESH)

    @pl.when(sends_hop)
    def _():
        pl.semaphore_signal(barrier, inc=1, device_id=(target, me), device_id_type=MESH)

    @pl.when(takes_hop)
    def _():
        pl.semaphore_signal(barrier, inc=1, device_id=(source, me), device_id_type=MESH)

    lax.fori_loop(1, REPLICAS, greet, 0)

    def span(index, size):
        return pl.ds(pl.multiple_of(index * size, size), size)

    def slopes(slot, rows):
        hidden = matmul(x[slot, rows, :], wu[slot])
        cdf = 0.5 * (1.0 + lax.erf(hidden * inv_root_two))
        density = jnp.exp(-0.5 * hidden * hidden) * inv_root_two_pi
        slope[slot, rows, :] = cdf + hidden * density
        return hidden * cdf

    def forward(index):
        rows = span(index, GROUP)
        act[rows, :] = slopes(home, rows).astype(BF)

    def transposes(slot):
        wdt[slot] = wd[slot].T
        wut[slot] = wu[slot].T

    for copy in loads[:3]:
        copy.wait()
    transposes(home)

    @pl.when(first)
    def _():
        forward(0)

    pl.semaphore_wait(barrier, REPLICAS + jnp.where(sends_hop, 1, 0) + jnp.where(takes_hop, 1, 0))

    @pl.when(gives_now)
    def _():
        for copy in gives:
            copy.start()

    def buffer_sketch():
        for copy in loads[3:]:
            copy.wait()
        up = su[...].T.astype(BF)
        zero_up = jnp.zeros_like(up)
        ssu[...] = jnp.concatenate([up, zero_up, zero_up, up], axis=1)
        down = sd[...].T.astype(BF)
        zero_down = jnp.zeros_like(down)
        ssd[...] = jnp.concatenate([down, zero_down, zero_down, down], axis=1)
        z[0 : D // 2, :] = matmul(gu[0 : D // 2, :].astype(BF), ssu[:, 0:128]) + matmul(
            gu[D // 2 : D, :].astype(BF), ssu[:, 128:256]
        )
        z[D // 2 : PACKED, :] = matmul(gd[0 : FF // 2, :].astype(BF), ssd[:, 0:128]) + matmul(
            gd[FF // 2 : FF, :].astype(BF), ssd[:, 128:256]
        )

    @pl.when(jnp.logical_not(first))
    def _():
        def step(index, carry):
            forward(index)
            return carry

        lax.fori_loop(0, GROUPS, step, 0)
        buffer_sketch()

    @pl.when(takes_now)
    def _():
        gives[0].wait_recv()
        gives[1].wait_recv()

        def step(index, carry):
            slopes(1, span(index, GROUP))
            return carry

        lax.fori_loop(0, GROUPS, step, 0)
        gives[2].wait_recv()
        transposes(1)

    @pl.when(takes_cot)
    def _():
        cot_load.wait()

    def hop(index):
        rows = span(index, PIECE)
        return remote(
            dy.at[2, rows, :], dy.at[0, rows, :], hop_send.at[index], hop_recv.at[index], (target, me)
        )

    def side(kind, index):
        rows = span(index, PIECE)
        ref = [dy.at[1, rows, :], dh.at[1, rows, :], dy.at[2, rows, :]][kind]
        return remote(ref, ref, side_send.at[kind, index], side_recv.at[kind, index], (partner, me))

    def layer(slot, index):
        rows = span(index, PIECE)
        dy_piece = dy[slot, rows, :]
        dh_piece = (matmul(dy_piece, wdt[slot]) * slope[slot, rows, :]).astype(BF)
        dy[slot + 1, rows, :] = (dy_piece.astype(F32) + matmul(dh_piece, wut[slot])).astype(BF)
        dh[slot, rows, :] = dh_piece

    def run_piece(index):
        @pl.when(takes_hop)
        def _():
            hop(index).wait_recv()

        @pl.when(upper)
        def _():
            layer(0, index)
            side(0, index).start()

        @pl.when(lower)
        def _():
            side(0, index).wait_recv()

        @pl.when(gives_now)
        def _():
            side(1, index).wait_recv()

        @pl.when(jnp.logical_or(takes_now, jnp.logical_and(ends, lower)))
        def _():
            layer(1, index)

        @pl.when(sends_hop)
        def _():
            hop(index).start()

        @pl.when(takes_now)
        def _():
            side(1, index).start()
            side(2, index).start()

    def sketch(index):
        rows = span(index, GROUP)
        x_part = x[home, rows, :]
        act_part = act[rows, :]
        up = matmul(dh[home, rows, :], ssu[...]).astype(BF)
        down = matmul(dy[home, rows, :], ssd[...]).astype(BF)
        z[0 : D // 2, :] += contract_first(x_part[:, 0 : D // 2], up[:, 0:128]) + contract_first(
            x_part[:, D // 2 : D], up[:, 128:256]
        )
        z[D // 2 : PACKED, :] += contract_first(act_part[:, 0 : FF // 2], down[:, 0:128]) + contract_first(
            act_part[:, FF // 2 : FF], down[:, 128:256]
        )

    def run_group(group, carry):
        def inner(piece, inner_carry):
            run_piece(group * PER_GROUP + piece)
            return inner_carry

        lax.fori_loop(0, PER_GROUP, inner, 0)

        @pl.when(jnp.logical_and(first, group < GROUPS - 1))
        def _():
            forward(jnp.minimum(group + 1, GROUPS - 1))

        @pl.when(jnp.logical_not(late))
        def _():
            sketch(group)

        return carry

    lax.fori_loop(0, GROUPS, run_group, 0)

    @pl.when(first)
    def _():
        buffer_sketch()

    @pl.when(late)
    def _():
        def step(index, carry):
            sketch(index)
            return carry

        lax.fori_loop(0, GROUPS, step, 0)

    def block_rows(index):
        return pl.ds(pl.multiple_of(index * BLOCK, BLOCK), BLOCK)

    zbf[...] = z[...].astype(BF)

    def scatter(step):
        peer = lax.rem(me + step, REPLICAS)
        return remote(zbf.at[block_rows(peer), :], rs.at[me], rs_send.at[step], rs_recv.at[me], (pos, peer))

    def gather(step):
        peer = lax.rem(me + step, REPLICAS)
        mine = block_rows(me)
        return remote(ag.at[mine, :], ag.at[mine, :], ag_send.at[step], ag_recv.at[me], (pos, peer))

    def scatter_start(step, carry):
        scatter(step).start()
        return carry

    def scatter_wait(step, carry):
        origin = lax.rem(me + step, REPLICAS)
        remote(
            zbf.at[block_rows(me), :], rs.at[origin], rs_send.at[step], rs_recv.at[origin], (pos, origin)
        ).wait_recv()
        return carry + rs[origin].astype(F32)

    def gather_start(step, carry):
        gather(step).start()
        return carry

    def gather_wait(step, carry):
        origin = lax.rem(me + step, REPLICAS)
        theirs = block_rows(origin)
        remote(
            ag.at[theirs, :], ag.at[theirs, :], ag_send.at[step], ag_recv.at[origin], (pos, origin)
        ).wait_recv()
        return carry

    def sends_done(step, carry):
        scatter(step).wait_send()
        gather(step).wait_send()
        return carry

    lax.fori_loop(1, REPLICAS, scatter_start, 0)
    gu[...] += contract_first(x[home], dh[home])
    gd[...] += contract_first(act[...], dy[home])
    outs = [
        pltpu.make_async_copy(src, dst, out_sem.at[k])
        for k, (src, dst) in enumerate([(gu, usum_hbm), (gd, dsum_hbm), (dy.at[home + 1], dx_hbm)])
    ]
    outs[0].start()
    outs[1].start()
    total = lax.fori_loop(1, REPLICAS, scatter_wait, z[block_rows(me), :])
    ag[block_rows(me), :] = total.astype(BF)
    lax.fori_loop(1, REPLICAS, gather_start, 0)

    def pieces_done(index, carry):
        @pl.when(upper)
        def _():
            side(0, index).wait_send()

        @pl.when(takes_now)
        def _():
            side(1, index).wait_send()
            side(2, index).wait_send()

        @pl.when(gives_now)
        def _():
            side(2, index).wait_recv()

        @pl.when(sends_hop)
        def _():
            hop(index).wait_send()

        return carry

    lax.fori_loop(0, PIECES, pieces_done, 0)

    @pl.when(gives_now)
    def _():
        for copy in gives:
            copy.wait_send()

    outs[2].start()
    lax.fori_loop(1, REPLICAS, gather_wait, 0)
    tot_up[0 : D // 2, :] = ag[0 : D // 2, 0:RANK]
    tot_up[D // 2 : D, :] = ag[0 : D // 2, RANK : 2 * RANK]
    tot_down[0 : FF // 2, :] = ag[D // 2 : PACKED, 0:RANK]
    tot_down[FF // 2 : FF, :] = ag[D // 2 : PACKED, RANK : 2 * RANK]
    lax.fori_loop(1, REPLICAS, sends_done, 0)
    for copy in outs:
        copy.wait()


CHUNKS = 4


def update_kernel(
    tot_up, tot_down, su, sd, usum, dsum, dx_in, new_up, new_down, up_part, down_part, dx_out,
    nu, nd, dx, in_sem, out_sem,
):
    me = lax.axis_index("dp")
    ub = D // CHUNKS
    db = FF // CHUNKS
    rb = ROWS // CHUNKS
    triples = []
    for chunk in range(CHUNKS):
        triples.append((usum, nu, new_up, pl.ds(chunk * ub, ub)))
        triples.append((dsum, nd, new_down, pl.ds(chunk * db, db)))
    for chunk in range(CHUNKS):
        triples.append((dx_in, dx, dx_out, pl.ds(chunk * rb, rb)))
    fetch = [
        pltpu.make_async_copy(src.at[rows, :], buf.at[rows, :], in_sem.at[k])
        for k, (src, buf, _, rows) in enumerate(triples)
    ]
    store = [
        pltpu.make_async_copy(buf.at[rows, :], dst.at[rows, :], out_sem.at[k])
        for k, (_, buf, dst, rows) in enumerate(triples)
    ]
    for copy in fetch:
        copy.start()
    ssu = (su[...] * (1.0 / REPLICAS)).astype(BF)
    ssd = (sd[...] * (1.0 / REPLICAS)).astype(BF)
    up_rows = D // REPLICAS
    down_rows = FF // REPLICAS
    up_part[...] = matmul(tot_up[pl.ds(pl.multiple_of(me * up_rows, up_rows), up_rows), :], ssu)
    down_part[...] = matmul(tot_down[pl.ds(pl.multiple_of(me * down_rows, down_rows), down_rows), :], ssd)
    for k, (src, buf, _, rows) in enumerate(triples):
        fetch[k].wait()
        if k < 2 * CHUNKS:
            total, sketch = (tot_up, ssu) if k % 2 == 0 else (tot_down, ssd)
            buf[rows, :] = buf[rows, :] - matmul(total[rows, :], sketch)
        store[k].start()
    for copy in store:
        copy.wait()


def on_device(
    stored_inputs, cotangent, up_weight, down_weight, up_buffer, down_buffer, up_sketch, down_sketch
):
    any_spec = pl.BlockSpec(memory_space=pl.ANY)
    vmem = pl.BlockSpec(memory_space=pltpu.VMEM)
    x = stored_inputs.reshape(ROWS, D)
    cot = cotangent.reshape(ROWS, D)
    sketch_up = jnp.swapaxes(up_sketch[0], 0, 1)
    sketch_down = jnp.swapaxes(down_sketch[0], 0, 1)
    dx, usum, dsum, tot_up, tot_down = pl.pallas_call(
        relay_kernel,
        name="relay",
        out_shape=(
            jax.ShapeDtypeStruct((ROWS, D), BF),
            jax.ShapeDtypeStruct((D, FF), F32),
            jax.ShapeDtypeStruct((FF, D), F32),
            jax.ShapeDtypeStruct((D, RANK), BF),
            jax.ShapeDtypeStruct((FF, RANK), BF),
        ),
        in_specs=[any_spec] * 8,
        out_specs=(any_spec, any_spec, any_spec, vmem, vmem),
        scratch_shapes=[
            pltpu.VMEM((2, ROWS, D), BF),
            pltpu.VMEM((3, ROWS, D), BF),
            pltpu.VMEM((2, ROWS, FF), BF),
            pltpu.VMEM((ROWS, FF), BF),
            pltpu.VMEM((D, FF), F32),
            pltpu.VMEM((FF, D), F32),
            pltpu.VMEM((2, ROWS, FF), F32),
            pltpu.VMEM((2, D, FF), BF),
            pltpu.VMEM((2, FF, D), BF),
            pltpu.VMEM((2, FF, D), BF),
            pltpu.VMEM((2, D, FF), BF),
            pltpu.VMEM((RANK, FF), F32),
            pltpu.VMEM((RANK, D), F32),
            pltpu.VMEM((FF, 4 * RANK), BF),
            pltpu.VMEM((D, 4 * RANK), BF),
            pltpu.VMEM((PACKED, 2 * RANK), F32),
            pltpu.VMEM((PACKED, 2 * RANK), BF),
            pltpu.VMEM((REPLICAS, BLOCK, 2 * RANK), BF),
            pltpu.VMEM((PACKED, 2 * RANK), BF),
            pltpu.SemaphoreType.DMA((8,)),
            pltpu.SemaphoreType.DMA((3,)),
            pltpu.SemaphoreType.DMA((3,)),
            pltpu.SemaphoreType.DMA((3,)),
            pltpu.SemaphoreType.DMA((PIECES,)),
            pltpu.SemaphoreType.DMA((PIECES,)),
            pltpu.SemaphoreType.DMA((3, PIECES)),
            pltpu.SemaphoreType.DMA((3, PIECES)),
            pltpu.SemaphoreType.DMA((REPLICAS,)),
            pltpu.SemaphoreType.DMA((REPLICAS,)),
            pltpu.SemaphoreType.DMA((REPLICAS,)),
            pltpu.SemaphoreType.DMA((REPLICAS,)),
        ],
        compiler_params=pltpu.CompilerParams(
            collective_id=0, has_side_effects=True, vmem_limit_bytes=60 * 2**20
        ),
    )(x, cot, up_weight[0], down_weight[0], up_buffer[0, 0], down_buffer[0, 0], sketch_up, sketch_down)
    new_up, new_down, up_part, down_part, grads = pl.pallas_call(
        update_kernel,
        name="update",
        out_shape=(
            jax.ShapeDtypeStruct((D, FF), F32),
            jax.ShapeDtypeStruct((FF, D), F32),
            jax.ShapeDtypeStruct((D // REPLICAS, FF), F32),
            jax.ShapeDtypeStruct((FF // REPLICAS, D), F32),
            jax.ShapeDtypeStruct((ROWS, D), BF),
        ),
        in_specs=[vmem] * 4 + [any_spec] * 3,
        out_specs=(any_spec, any_spec, vmem, vmem, any_spec),
        scratch_shapes=[
            pltpu.VMEM((D, FF), F32),
            pltpu.VMEM((FF, D), F32),
            pltpu.VMEM((ROWS, D), BF),
            pltpu.SemaphoreType.DMA((3 * CHUNKS,)),
            pltpu.SemaphoreType.DMA((3 * CHUNKS,)),
        ],
        compiler_params=pltpu.CompilerParams(vmem_limit_bytes=60 * 2**20),
    )(tot_up, tot_down, sketch_up, sketch_down, usum, dsum, dx)
    return (
        grads.reshape(1, 2, ROWS // 2, D),
        new_up[None, None],
        new_down[None, None],
        up_part[None],
        down_part[None],
    )


def solution(mesh):
    return jax.shard_map(
        on_device,
        mesh=mesh,
        in_specs=(
            P("pipe", None, "dp", None),
            P(None, "dp", None),
            P("pipe", None, None),
            P("pipe", None, None),
            P("pipe", "dp", None, None),
            P("pipe", "dp", None, None),
            P("pipe", None, None),
            P("pipe", None, None),
        ),
        out_specs=(
            P("pipe", None, "dp", None),
            P("pipe", "dp", None, None),
            P("pipe", "dp", None, None),
            P("pipe", "dp", None),
            P("pipe", "dp", None),
        ),
        check_vma=False,
    )
```

time: 126 us -> 105 us (0.83); the launches traced: 124 us -> 104 us
  Pallas kernels: 114 us -> 104 us
  local copies, waits for them, and re-layouts: 9.02 us -> 0 us
    pallas_call x1, Pallas kernels: 111 us -> 97.8 us  [on_device(): pl.pallas_call(relay_kernel, name='relay', out_shape=(jax.ShapeDtypeStruc...]
    unnamed x12 -> x0, local copies, waits for them, and re-layouts: 9.02 us -> none
    pallas_call x1, Pallas kernels: 3.23 us -> 5.99 us  [on_device(): pl.pallas_call(update_kernel, name='update', out_shape=(jax.ShapeDtypeStr...]
where the time goes in v2:
time: 105 us; the launch traced here: 104 us
  Pallas kernels  104 us (99%)
    pallas_call x1, Pallas kernels, on_device(): pl.pallas_call(relay_kernel, name='relay', out_shape=(jax.ShapeDtypeStruc...  97.8 us
    pallas_call x1, Pallas kernels, on_device(): pl.pallas_call(update_kernel, name='update', out_shape=(jax.ShapeDtypeStr...  5.99 us

profile of v2, /device:TPU:24, one launch (start us, length us, event | category | flops | bytes accessed | tf_op | source)
XLA Modules:
  0.0 104.4 jit_solution(15188612570804698204)
XLA Ops:
  0.6 97.8 %relay.1 = (bf16[1024,512]{1,0:T(8,128)(2,1)}, f32[512,1024]{1,0:T(8,128)}, f32[1024,512]{1,0:T(8,128)}, bf16[512,64]{1,0:T(8,128)(2,1)}, bf16[1024,64]{1,0:T(8,128)(2,1)}) custom-call(bf16[1024,512]{1,0:T(8,128)(2,1)} %bitcast.19, bf16[1024,512]{1,0:T(8,128)(2,1)} %bitcast.20, bf16[512,1024]{1,0:T(8,128)(2,1)} %bitcast.21, bf16[1024,512]{1,0:T(8,128)(2,1)} %bitcast.22, ...), custom_call_target="tpu_custom_call" | custom-call | tf_op jit(solution)/shard_map/relay/pallas_call | solution.py:439
  98.4 6.0 %update.1 = (f32[512,1024]{1,0:T(8,128)}, f32[1024,512]{1,0:T(8,128)}, f32[32,1024]{1,0:T(8,128)}, f32[64,512]{1,0:T(8,128)}, bf16[1024,512]{1,0:T(8,128)(2,1)}) custom-call(bf16[512,64]{1,0:T(8,128)(2,1)} %get-tuple-element.15.tot_up, bf16[1024,64]{1,0:T(8,128)(2,1)} %get-tuple-element.16.tot_down, f32[64,1024]{1,0:T(8,128)} %bitcast.24, ...), custom_call_target="tpu_custom_call" | custom-call | tf_op jit(solution)/shard_map/update/pallas_call | solution.py:488

commit v3 on v2

--- a/solution.py
+++ b/solution.py
@@ -10,6 +10,8 @@
 F32 = jnp.float32
 SECTIONS = 16
 REPLICAS = 16
+DP_Y = 4
+DP_Z = 4
 D = 512
 FF = 1024
 RANK = 64
@@ -48,7 +50,7 @@
 def relay_kernel(
     x_hbm, cot_hbm, wu_hbm, wd_hbm, ub_hbm, db_hbm, us_hbm, ds_hbm,
     dx_hbm, usum_hbm, dsum_hbm, tot_up, tot_down,
-    x, dy, dh, act, gu, gd, slope, wu, wd, wut, wdt, su, sd, ssu, ssd,
+    x, hop_in, hop_out, book, act, gu, gd, slope, wu, wd, wut, wdt, su, sd, ssu, ssd,
     z, zbf, rs, ag,
     load_sem, out_sem, give_send, give_recv, hop_send, hop_recv,
     side_send, side_recv, rs_send, rs_recv, ag_send, ag_recv,
@@ -68,7 +70,9 @@
     takes_hop = jnp.logical_and(upper, jnp.logical_not(first))
     gives_now = jnp.logical_and(mid, lower)
     takes_now = jnp.logical_and(mid, upper)
-    late = jnp.logical_or(first, takes_now)
+    inner = jnp.logical_or(me // 4 == 1, me // 4 == 2)
+    slow_start = jnp.logical_and(first, inner)
+    late = jnp.logical_or(slow_start, takes_now)
     partner = 2 * chip + 1 - core
     target = 2 * jnp.maximum(chip - 1, 0) + 1
     ahead = jnp.minimum(chip + 1, CHIPS - 1)
@@ -88,7 +92,7 @@
             ]
         )
     ]
-    cot_load = pltpu.make_async_copy(cot_hbm, dy.at[0], load_sem.at[7])
+    cot_load = pltpu.make_async_copy(cot_hbm, hop_in, load_sem.at[7])
     takes_cot = jnp.logical_and(first, upper)
     gives = [
         remote(src, dst, give_send.at[k], give_recv.at[k], (partner, me))
@@ -179,6 +183,9 @@
             return carry
 
         lax.fori_loop(0, GROUPS, step, 0)
+
+    @pl.when(jnp.logical_not(slow_start))
+    def _():
         buffer_sketch()
 
     @pl.when(takes_now)
@@ -201,58 +208,69 @@
     def hop(index):
         rows = span(index, PIECE)
         return remote(
-            dy.at[2, rows, :], dy.at[0, rows, :], hop_send.at[index], hop_recv.at[index], (target, me)
-        )
-
-    def side(kind, index):
+            hop_out.at[rows, :], hop_in.at[rows, :], hop_send.at[index], hop_recv.at[index], (target, me)
+        )
+
+    def side(index):
+        ref = book.at[1, span(index, PIECE), :]
+        return remote(ref, ref, side_send.at[index], side_recv.at[index], (partner, me))
+
+    def side_dy(index):
+        ref = book.at[1, span(index, PIECE), 0:D]
+        return remote(ref, ref, side_send.at[index], side_recv.at[index], (partner, me))
+
+    def layer(slot, rows, dy_piece):
+        dh_piece = (matmul(dy_piece, wdt[slot]) * slope[slot, rows, :]).astype(BF)
+        dx_piece = (dy_piece.astype(F32) + matmul(dh_piece, wut[slot])).astype(BF)
+        book[slot, rows, D : 2 * D] = dx_piece
+        book[slot, rows, 2 * D : 2 * D + FF] = dh_piece
+        return dx_piece
+
+    def run_mid(index, carry):
+        hop(index).wait_recv()
         rows = span(index, PIECE)
-        ref = [dy.at[1, rows, :], dh.at[1, rows, :], dy.at[2, rows, :]][kind]
-        return remote(ref, ref, side_send.at[kind, index], side_recv.at[kind, index], (partner, me))
-
-    def layer(slot, index):
+        dy_piece = hop_in[rows, :]
+        mid_piece = layer(0, rows, dy_piece)
+        hop_out[rows, :] = layer(1, rows, mid_piece)
+        hop(index).start()
+        book[0, rows, 0:D] = dy_piece
+        book[1, rows, 0:D] = mid_piece
+        side(index).start()
+        return carry
+
+    def run_piece(index):
         rows = span(index, PIECE)
-        dy_piece = dy[slot, rows, :]
-        dh_piece = (matmul(dy_piece, wdt[slot]) * slope[slot, rows, :]).astype(BF)
-        dy[slot + 1, rows, :] = (dy_piece.astype(F32) + matmul(dh_piece, wut[slot])).astype(BF)
-        dh[slot, rows, :] = dh_piece
-
-    def run_piece(index):
-        @pl.when(takes_hop)
-        def _():
-            hop(index).wait_recv()
 
         @pl.when(upper)
         def _():
-            layer(0, index)
-            side(0, index).start()
-
-        @pl.when(lower)
-        def _():
-            side(0, index).wait_recv()
+            @pl.when(takes_hop)
+            def _():
+                hop(index).wait_recv()
+
+            dy_piece = hop_in[rows, :]
+            book[0, rows, 0:D] = dy_piece
+            book[1, rows, 0:D] = layer(0, rows, dy_piece)
+            side_dy(index).start()
 
         @pl.when(gives_now)
         def _():
-            side(1, index).wait_recv()
-
-        @pl.when(jnp.logical_or(takes_now, jnp.logical_and(ends, lower)))
-        def _():
-            layer(1, index)
-
-        @pl.when(sends_hop)
-        def _():
-            hop(index).start()
-
-        @pl.when(takes_now)
-        def _():
-            side(1, index).start()
-            side(2, index).start()
+            side(index).wait_recv()
+
+        @pl.when(jnp.logical_and(ends, lower))
+        def _():
+            side_dy(index).wait_recv()
+            hop_out[rows, :] = layer(1, rows, book[1, rows, 0:D])
+
+            @pl.when(first)
+            def _():
+                hop(index).start()
 
     def sketch(index):
         rows = span(index, GROUP)
         x_part = x[home, rows, :]
         act_part = act[rows, :]
-        up = matmul(dh[home, rows, :], ssu[...]).astype(BF)
-        down = matmul(dy[home, rows, :], ssd[...]).astype(BF)
+        up = matmul(book[home, rows, 2 * D : 2 * D + FF], ssu[...]).astype(BF)
+        down = matmul(book[home, rows, 0:D], ssd[...]).astype(BF)
         z[0 : D // 2, :] += contract_first(x_part[:, 0 : D // 2], up[:, 0:128]) + contract_first(
             x_part[:, D // 2 : D], up[:, 128:256]
         )
@@ -277,9 +295,15 @@
 
         return carry
 
-    lax.fori_loop(0, GROUPS, run_group, 0)
-
-    @pl.when(first)
+    @pl.when(takes_now)
+    def _():
+        lax.fori_loop(0, PIECES, run_mid, 0)
+
+    @pl.when(jnp.logical_not(takes_now))
+    def _():
+        lax.fori_loop(0, GROUPS, run_group, 0)
+
+    @pl.when(slow_start)
     def _():
         buffer_sketch()
 
@@ -296,69 +320,54 @@
 
     zbf[...] = z[...].astype(BF)
 
-    def scatter(step):
-        peer = lax.rem(me + step, REPLICAS)
-        return remote(zbf.at[block_rows(peer), :], rs.at[me], rs_send.at[step], rs_recv.at[me], (pos, peer))
-
-    def gather(step):
-        peer = lax.rem(me + step, REPLICAS)
-        mine = block_rows(me)
-        return remote(ag.at[mine, :], ag.at[mine, :], ag_send.at[step], ag_recv.at[me], (pos, peer))
-
-    def scatter_start(step, carry):
-        scatter(step).start()
-        return carry
-
-    def scatter_wait(step, carry):
-        origin = lax.rem(me + step, REPLICAS)
-        remote(
-            zbf.at[block_rows(me), :], rs.at[origin], rs_send.at[step], rs_recv.at[origin], (pos, origin)
-        ).wait_recv()
-        return carry + rs[origin].astype(F32)
-
-    def gather_start(step, carry):
-        gather(step).start()
-        return carry
-
-    def gather_wait(step, carry):
-        origin = lax.rem(me + step, REPLICAS)
-        theirs = block_rows(origin)
-        remote(
-            ag.at[theirs, :], ag.at[theirs, :], ag_send.at[step], ag_recv.at[origin], (pos, origin)
-        ).wait_recv()
-        return carry
-
-    def sends_done(step, carry):
-        scatter(step).wait_send()
-        gather(step).wait_send()
-        return carry
-
-    lax.fori_loop(1, REPLICAS, scatter_start, 0)
-    gu[...] += contract_first(x[home], dh[home])
-    gd[...] += contract_first(act[...], dy[home])
+    me_z = me // DP_Y
+    me_y = lax.rem(me, DP_Y)
+    peers = [
+        (DP_Y * lax.rem(me_z + dz, DP_Z) + lax.rem(me_y + dy, DP_Y), DP_Y * dz + dy)
+        for dy in (2, 1, 3, 0)
+        for dz in (2, 1, 3, 0)
+        if dz or dy
+    ]
+    mine = block_rows(me)
+
+    def scatter(peer, offset):
+        return remote(
+            zbf.at[block_rows(peer), :], rs.at[span(offset, BLOCK), :], rs_send, rs_recv, (pos, peer)
+        )
+
+    def gather(peer):
+        return remote(ag.at[mine, :], ag.at[mine, :], ag_send, ag_recv, (pos, peer))
+
+    def exchanged(send, recv):
+        everything = rs.at[BLOCK : REPLICAS * BLOCK, :]
+        return remote(everything, everything, send, recv, (pos, peers[0][0]))
+
+    for peer, offset in peers:
+        scatter(peer, offset).start()
+    gu[...] += contract_first(x[home], book[home, :, 2 * D : 2 * D + FF])
+    gd[...] += contract_first(act[...], book[home, :, 0:D])
     outs = [
         pltpu.make_async_copy(src, dst, out_sem.at[k])
-        for k, (src, dst) in enumerate([(gu, usum_hbm), (gd, dsum_hbm), (dy.at[home + 1], dx_hbm)])
+        for k, (src, dst) in enumerate([(gu, usum_hbm), (gd, dsum_hbm), (book.at[home, :, D : 2 * D], dx_hbm)])
     ]
     outs[0].start()
     outs[1].start()
-    total = lax.fori_loop(1, REPLICAS, scatter_wait, z[block_rows(me), :])
-    ag[block_rows(me), :] = total.astype(BF)
-    lax.fori_loop(1, REPLICAS, gather_start, 0)
+    exchanged(rs_send, rs_recv).wait_recv()
+    total = z[mine, :]
+    for _, offset in peers:
+        total += rs[offset * BLOCK : (offset + 1) * BLOCK, :].astype(F32)
+    ag[mine, :] = total.astype(BF)
+    for peer, _ in peers:
+        gather(peer).start()
 
     def pieces_done(index, carry):
-        @pl.when(upper)
-        def _():
-            side(0, index).wait_send()
-
         @pl.when(takes_now)
         def _():
-            side(1, index).wait_send()
-            side(2, index).wait_send()
-
-        @pl.when(gives_now)
-        def _():
-            side(2, index).wait_recv()
+            side(index).wait_send()
+
+        @pl.when(jnp.logical_and(ends, upper))
+        def _():
+            side_dy(index).wait_send()
 
         @pl.when(sends_hop)
         def _():
@@ -374,12 +383,13 @@
             copy.wait_send()
 
     outs[2].start()
-    lax.fori_loop(1, REPLICAS, gather_wait, 0)
+    exchanged(ag_send, ag_recv).wait_recv()
     tot_up[0 : D // 2, :] = ag[0 : D // 2, 0:RANK]
     tot_up[D // 2 : D, :] = ag[0 : D // 2, RANK : 2 * RANK]
     tot_down[0 : FF // 2, :] = ag[D // 2 : PACKED, 0:RANK]
     tot_down[FF // 2 : FF, :] = ag[D // 2 : PACKED, RANK : 2 * RANK]
-    lax.fori_loop(1, REPLICAS, sends_done, 0)
+    exchanged(rs_send, rs_recv).wait_send()
+    exchanged(ag_send, ag_recv).wait_send()
     for copy in outs:
         copy.wait()
 
@@ -388,19 +398,23 @@
 
 
 def update_kernel(
-    tot_up, tot_down, su, sd, usum, dsum, dx_in, new_up, new_down, up_part, down_part, dx_out,
-    nu, nd, dx, in_sem, out_sem,
+    tot_up_hbm, tot_down_hbm, su_hbm, sd_hbm, usum, dsum, dx_in,
+    new_up, new_down, up_part, down_part, dx_out,
+    tot_up, tot_down, su, sd, nu, nd, dx, pu, pd, in_sem, out_sem,
 ):
     me = lax.axis_index("dp")
     ub = D // CHUNKS
     db = FF // CHUNKS
     rb = ROWS // CHUNKS
+    small = [(tot_up_hbm, tot_up), (tot_down_hbm, tot_down), (su_hbm, su), (sd_hbm, sd)]
     triples = []
     for chunk in range(CHUNKS):
         triples.append((usum, nu, new_up, pl.ds(chunk * ub, ub)))
         triples.append((dsum, nd, new_down, pl.ds(chunk * db, db)))
     for chunk in range(CHUNKS):
         triples.append((dx_in, dx, dx_out, pl.ds(chunk * rb, rb)))
+    count = len(triples)
+    early = [pltpu.make_async_copy(src, dst, in_sem.at[count + k]) for k, (src, dst) in enumerate(small)]
     fetch = [
         pltpu.make_async_copy(src.at[rows, :], buf.at[rows, :], in_sem.at[k])
         for k, (src, buf, _, rows) in enumerate(triples)
@@ -409,14 +423,20 @@
         pltpu.make_async_copy(buf.at[rows, :], dst.at[rows, :], out_sem.at[k])
         for k, (_, buf, dst, rows) in enumerate(triples)
     ]
-    for copy in fetch:
+    store.append(pltpu.make_async_copy(pu, up_part, out_sem.at[count]))
+    store.append(pltpu.make_async_copy(pd, down_part, out_sem.at[count + 1]))
+    for copy in early + fetch:
         copy.start()
+    for copy in early:
+        copy.wait()
     ssu = (su[...] * (1.0 / REPLICAS)).astype(BF)
     ssd = (sd[...] * (1.0 / REPLICAS)).astype(BF)
     up_rows = D // REPLICAS
     down_rows = FF // REPLICAS
-    up_part[...] = matmul(tot_up[pl.ds(pl.multiple_of(me * up_rows, up_rows), up_rows), :], ssu)
-    down_part[...] = matmul(tot_down[pl.ds(pl.multiple_of(me * down_rows, down_rows), down_rows), :], ssd)
+    pu[...] = matmul(tot_up[pl.ds(pl.multiple_of(me * up_rows, up_rows), up_rows), :], ssu)
+    pd[...] = matmul(tot_down[pl.ds(pl.multiple_of(me * down_rows, down_rows), down_rows), :], ssd)
+    store[count].start()
+    store[count + 1].start()
     for k, (src, buf, _, rows) in enumerate(triples):
         fetch[k].wait()
         if k < 2 * CHUNKS:
@@ -450,8 +470,9 @@
         out_specs=(any_spec, any_spec, any_spec, vmem, vmem),
         scratch_shapes=[
             pltpu.VMEM((2, ROWS, D), BF),
-            pltpu.VMEM((3, ROWS, D), BF),
-            pltpu.VMEM((2, ROWS, FF), BF),
+            pltpu.VMEM((ROWS, D), BF),
+            pltpu.VMEM((ROWS, D), BF),
+            pltpu.VMEM((2, ROWS, 2 * D + FF), BF),
             pltpu.VMEM((ROWS, FF), BF),
             pltpu.VMEM((D, FF), F32),
             pltpu.VMEM((FF, D), F32),
@@ -466,7 +487,7 @@
             pltpu.VMEM((D, 4 * RANK), BF),
             pltpu.VMEM((PACKED, 2 * RANK), F32),
             pltpu.VMEM((PACKED, 2 * RANK), BF),
-            pltpu.VMEM((REPLICAS, BLOCK, 2 * RANK), BF),
+            pltpu.VMEM((REPLICAS * BLOCK, 2 * RANK), BF),
             pltpu.VMEM((PACKED, 2 * RANK), BF),
             pltpu.SemaphoreType.DMA((8,)),
             pltpu.SemaphoreType.DMA((3,)),
@@ -474,12 +495,12 @@
             pltpu.SemaphoreType.DMA((3,)),
             pltpu.SemaphoreType.DMA((PIECES,)),
             pltpu.SemaphoreType.DMA((PIECES,)),
-            pltpu.SemaphoreType.DMA((3, PIECES)),
-            pltpu.SemaphoreType.DMA((3, PIECES)),
-            pltpu.SemaphoreType.DMA((REPLICAS,)),
-            pltpu.SemaphoreType.DMA((REPLICAS,)),
-            pltpu.SemaphoreType.DMA((REPLICAS,)),
-            pltpu.SemaphoreType.DMA((REPLICAS,)),
+            pltpu.SemaphoreType.DMA((PIECES,)),
+            pltpu.SemaphoreType.DMA((PIECES,)),
+            pltpu.SemaphoreType.DMA,
+            pltpu.SemaphoreType.DMA,
+            pltpu.SemaphoreType.DMA,
+            pltpu.SemaphoreType.DMA,
         ],
         compiler_params=pltpu.CompilerParams(
             collective_id=0, has_side_effects=True, vmem_limit_bytes=60 * 2**20
@@ -495,14 +516,20 @@
             jax.ShapeDtypeStruct((FF // REPLICAS, D), F32),
             jax.ShapeDtypeStruct((ROWS, D), BF),
         ),
-        in_specs=[vmem] * 4 + [any_spec] * 3,
-        out_specs=(any_spec, any_spec, vmem, vmem, any_spec),
+        in_specs=[any_spec] * 7,
+        out_specs=(any_spec,) * 5,
         scratch_shapes=[
+            pltpu.VMEM((D, RANK), BF),
+            pltpu.VMEM((FF, RANK), BF),
+            pltpu.VMEM((RANK, FF), F32),
+            pltpu.VMEM((RANK, D), F32),
             pltpu.VMEM((D, FF), F32),
             pltpu.VMEM((FF, D), F32),
             pltpu.VMEM((ROWS, D), BF),
-            pltpu.SemaphoreType.DMA((3 * CHUNKS,)),
-            pltpu.SemaphoreType.DMA((3 * CHUNKS,)),
+            pltpu.VMEM((D // REPLICAS, FF), F32),
+            pltpu.VMEM((FF // REPLICAS, D), F32),
+            pltpu.SemaphoreType.DMA((3 * CHUNKS + 4,)),
+            pltpu.SemaphoreType.DMA((3 * CHUNKS + 2,)),
         ],
         compiler_params=pltpu.CompilerParams(vmem_limit_bytes=60 * 2**20),
     )(tot_up, tot_down, sketch_up, sketch_down, usum, dsum, dx)

time: 105 us -> 99 us (0.943)
  Pallas kernels: 104 us -> 98.3 us
    pallas_call x1, Pallas kernels: 97.8 us -> 93.6 us  [on_device(): pl.pallas_call(relay_kernel, name='relay', out_shape=(jax.ShapeDtypeStruc...]
    pallas_call x1, Pallas kernels: 5.99 us -> 4.73 us  [on_device(): pl.pallas_call(update_kernel, name='update', out_shape=(jax.ShapeDtypeStr...]
where the time goes in v3:
time: 99 us
  Pallas kernels  98.3 us (99%)
    pallas_call x1, Pallas kernels, on_device(): pl.pallas_call(relay_kernel, name='relay', out_shape=(jax.ShapeDtypeStruc...  93.6 us
    pallas_call x1, Pallas kernels, on_device(): pl.pallas_call(update_kernel, name='update', out_shape=(jax.ShapeDtypeStr...  4.73 us

profile of v3, /device:TPU:24, one launch (start us, length us, event | category | flops | bytes accessed | tf_op | source)
XLA Modules:
  0.0 99.0 jit_solution(13411203070376326997)
XLA Ops:
  0.6 93.6 %relay.1 = (bf16[1024,512]{1,0:T(8,128)(2,1)}, f32[512,1024]{1,0:T(8,128)}, f32[1024,512]{1,0:T(8,128)}, bf16[512,64]{1,0:T(8,128)(2,1)}, bf16[1024,64]{1,0:T(8,128)(2,1)}) custom-call(bf16[1024,512]{1,0:T(8,128)(2,1)} %bitcast.19, bf16[1024,512]{1,0:T(8,128)(2,1)} %bitcast.20, bf16[512,1024]{1,0:T(8,128)(2,1)} %bitcast.21, bf16[1024,512]{1,0:T(8,128)(2,1)} %bitcast.22, ...), custom_call_target="tpu_custom_call" | custom-call | tf_op jit(solution)/shard_map/relay/pallas_call | solution.py:459
  94.2 4.7 %update.1 = (f32[512,1024]{1,0:T(8,128)}, f32[1024,512]{1,0:T(8,128)}, f32[32,1024]{1,0:T(8,128)}, f32[64,512]{1,0:T(8,128)}, bf16[1024,512]{1,0:T(8,128)(2,1)}) custom-call(bf16[512,64]{1,0:T(8,128)(2,1)} %get-tuple-element.15.tot_up_hbm, bf16[1024,64]{1,0:T(8,128)(2,1)} %get-tuple-element.16.tot_down_hbm, f32[64,1024]{1,0:T(8,128)} %bitcast.24, ...), custom_call_target="tpu_custom_call" | custom-call | tf_op jit(solution)/shard_map/update/pallas_call | solution.py:509

commit v4 on v3

--- a/solution.py
+++ b/solution.py
@@ -53,7 +53,7 @@
     x, hop_in, hop_out, book, act, gu, gd, slope, wu, wd, wut, wdt, su, sd, ssu, ssd,
     z, zbf, rs, ag,
     load_sem, out_sem, give_send, give_recv, hop_send, hop_recv,
-    side_send, side_recv, rs_send, rs_recv, ag_send, ag_recv,
+    side_send, side_recv, rs_send, rs_recv, ag_send, ag_recv, ready,
 ):
     pos = lax.axis_index("pipe")
     me = lax.axis_index("dp")
@@ -110,22 +110,23 @@
 
     barrier = pltpu.get_barrier_semaphore()
 
-    def greet(step, carry):
-        peer = lax.rem(me + step, REPLICAS)
+    me_z = me // DP_Y
+    me_y = lax.rem(me, DP_Y)
+    row = [DP_Y * me_z + lax.rem(me_y + dy, DP_Y) for dy in range(1, DP_Y)]
+    column = [DP_Y * lax.rem(me_z + dz, DP_Z) + me_y for dz in range(1, DP_Z)]
+
+    pl.semaphore_signal(barrier, inc=1, device_id=(partner, me), device_id_type=MESH)
+
+    @pl.when(sends_hop)
+    def _():
+        pl.semaphore_signal(barrier, inc=1, device_id=(target, me), device_id_type=MESH)
+
+    @pl.when(takes_hop)
+    def _():
+        pl.semaphore_signal(barrier, inc=1, device_id=(source, me), device_id_type=MESH)
+
+    for peer in row + column:
         pl.semaphore_signal(barrier, inc=1, device_id=(pos, peer), device_id_type=MESH)
-        return carry
-
-    pl.semaphore_signal(barrier, inc=1, device_id=(partner, me), device_id_type=MESH)
-
-    @pl.when(sends_hop)
-    def _():
-        pl.semaphore_signal(barrier, inc=1, device_id=(target, me), device_id_type=MESH)
-
-    @pl.when(takes_hop)
-    def _():
-        pl.semaphore_signal(barrier, inc=1, device_id=(source, me), device_id_type=MESH)
-
-    lax.fori_loop(1, REPLICAS, greet, 0)
 
     def span(index, size):
         return pl.ds(pl.multiple_of(index * size, size), size)
@@ -153,7 +154,10 @@
     def _():
         forward(0)
 
-    pl.semaphore_wait(barrier, REPLICAS + jnp.where(sends_hop, 1, 0) + jnp.where(takes_hop, 1, 0))
+    greeted = 1 + len(row) + len(column)
+    pl.semaphore_wait(barrier, greeted + jnp.where(sends_hop, 1, 0) + jnp.where(takes_hop, 1, 0))
+    for peer in row:
+        pl.semaphore_signal(ready, inc=1, device_id=(pos, peer), device_id_type=MESH)
 
     @pl.when(gives_now)
     def _():
@@ -320,8 +324,6 @@
 
     zbf[...] = z[...].astype(BF)
 
-    me_z = me // DP_Y
-    me_y = lax.rem(me, DP_Y)
     peers = [
         (DP_Y * lax.rem(me_z + dz, DP_Z) + lax.rem(me_y + dy, DP_Y), DP_Y * dz + dy)
         for dy in (2, 1, 3, 0)
@@ -342,6 +344,7 @@
         everything = rs.at[BLOCK : REPLICAS * BLOCK, :]
         return remote(everything, everything, send, recv, (pos, peers[0][0]))
 
+    pl.semaphore_wait(ready, len(row))
     for peer, offset in peers:
         scatter(peer, offset).start()
     gu[...] += contract_first(x[home], book[home, :, 2 * D : 2 * D + FF])
@@ -394,7 +397,7 @@
         copy.wait()
 
 
-CHUNKS = 4
+CHUNKS = 2
 
 
 def update_kernel(
@@ -501,6 +504,7 @@
             pltpu.SemaphoreType.DMA,
             pltpu.SemaphoreType.DMA,
             pltpu.SemaphoreType.DMA,
+            pltpu.SemaphoreType.REGULAR,
         ],
         compiler_params=pltpu.CompilerParams(
             collective_id=0, has_side_effects=True, vmem_limit_bytes=60 * 2**20

time: 99 us -> 98.1 us (level)
  no operation moved by 1% of the time
where the time goes in v4:
time: 98.1 us; the launch traced here: 98 us
  Pallas kernels  97.4 us (99%)
    pallas_call x1, Pallas kernels, on_device(): pl.pallas_call(relay_kernel, name='relay', out_shape=(jax.ShapeDtypeStruc...  93.1 us
    pallas_call x1, Pallas kernels, on_device(): pl.pallas_call(update_kernel, name='update', out_shape=(jax.ShapeDtypeStr...  4.27 us

profile of v4, /device:TPU:24, one launch (start us, length us, event | category | flops | bytes accessed | tf_op | source)
XLA Modules:
  0.0 98.0 jit_solution(5740055490522009238)
XLA Ops:
  0.6 93.1 %relay.1 = (bf16[1024,512]{1,0:T(8,128)(2,1)}, f32[512,1024]{1,0:T(8,128)}, f32[1024,512]{1,0:T(8,128)}, bf16[512,64]{1,0:T(8,128)(2,1)}, bf16[1024,64]{1,0:T(8,128)(2,1)}) custom-call(bf16[1024,512]{1,0:T(8,128)(2,1)} %bitcast.19, bf16[1024,512]{1,0:T(8,128)(2,1)} %bitcast.20, bf16[512,1024]{1,0:T(8,128)(2,1)} %bitcast.21, bf16[1024,512]{1,0:T(8,128)(2,1)} %bitcast.22, ...), custom_call_target="tpu_custom_call" | custom-call | tf_op jit(solution)/shard_map/relay/pallas_call | solution.py:462
  93.8 4.3 %update.1 = (f32[512,1024]{1,0:T(8,128)}, f32[1024,512]{1,0:T(8,128)}, f32[32,1024]{1,0:T(8,128)}, f32[64,512]{1,0:T(8,128)}, bf16[1024,512]{1,0:T(8,128)(2,1)}) custom-call(bf16[512,64]{1,0:T(8,128)(2,1)} %get-tuple-element.15.tot_up_hbm, bf16[1024,64]{1,0:T(8,128)(2,1)} %get-tuple-element.16.tot_down_hbm, f32[64,1024]{1,0:T(8,128)} %bitcast.24, ...), custom_call_target="tpu_custom_call" | custom-call | tf_op jit(solution)/shard_map/update/pallas_call | solution.py:513

commit v5 on v4

--- a/solution.py
+++ b/solution.py
@@ -49,7 +49,7 @@
 
 def relay_kernel(
     x_hbm, cot_hbm, wu_hbm, wd_hbm, ub_hbm, db_hbm, us_hbm, ds_hbm,
-    dx_hbm, usum_hbm, dsum_hbm, tot_up, tot_down,
+    dx_hbm, usum_hbm, dsum_hbm, tot_hbm,
     x, hop_in, hop_out, book, act, gu, gd, slope, wu, wd, wut, wdt, su, sd, ssu, ssd,
     z, zbf, rs, ag,
     load_sem, out_sem, give_send, give_recv, hop_send, hop_recv,
@@ -150,9 +150,27 @@
         copy.wait()
     transposes(home)
 
+    def layer(slot, rows, dy_piece):
+        dh_piece = (matmul(dy_piece, wdt[slot]) * slope[slot, rows, :]).astype(BF)
+        dx_piece = (dy_piece.astype(F32) + matmul(dh_piece, wut[slot])).astype(BF)
+        book[slot, rows, D : 2 * D] = dx_piece
+        book[slot, rows, 2 * D : 2 * D + FF] = dh_piece
+        return dx_piece
+
+    def upper_layer(index):
+        rows = span(index, PIECE)
+        dy_piece = hop_in[rows, :]
+        book[0, rows, 0:D] = dy_piece
+        book[1, rows, 0:D] = layer(0, rows, dy_piece)
+
     @pl.when(first)
     def _():
         forward(0)
+
+    @pl.when(takes_cot)
+    def _():
+        cot_load.wait()
+        upper_layer(0)
 
     greeted = 1 + len(row) + len(column)
     pl.semaphore_wait(barrier, greeted + jnp.where(sends_hop, 1, 0) + jnp.where(takes_hop, 1, 0))
@@ -205,10 +223,6 @@
         gives[2].wait_recv()
         transposes(1)
 
-    @pl.when(takes_cot)
-    def _():
-        cot_load.wait()
-
     def hop(index):
         rows = span(index, PIECE)
         return remote(
@@ -222,13 +236,6 @@
     def side_dy(index):
         ref = book.at[1, span(index, PIECE), 0:D]
         return remote(ref, ref, side_send.at[index], side_recv.at[index], (partner, me))
-
-    def layer(slot, rows, dy_piece):
-        dh_piece = (matmul(dy_piece, wdt[slot]) * slope[slot, rows, :]).astype(BF)
-        dx_piece = (dy_piece.astype(F32) + matmul(dh_piece, wut[slot])).astype(BF)
-        book[slot, rows, D : 2 * D] = dx_piece
-        book[slot, rows, 2 * D : 2 * D + FF] = dh_piece
-        return dx_piece
 
     def run_mid(index, carry):
         hop(index).wait_recv()
@@ -251,9 +258,10 @@
             def _():
                 hop(index).wait_recv()
 
-            dy_piece = hop_in[rows, :]
-            book[0, rows, 0:D] = dy_piece
-            book[1, rows, 0:D] = layer(0, rows, dy_piece)
+            @pl.when(jnp.logical_or(takes_hop, index > 0))
+            def _():
+                upper_layer(index)
+
             side_dy(index).start()
 
         @pl.when(gives_now)
@@ -351,7 +359,7 @@
     gd[...] += contract_first(act[...], book[home, :, 0:D])
     outs = [
         pltpu.make_async_copy(src, dst, out_sem.at[k])
-        for k, (src, dst) in enumerate([(gu, usum_hbm), (gd, dsum_hbm), (book.at[home, :, D : 2 * D], dx_hbm)])
+        for k, (src, dst) in enumerate([(gu, usum_hbm), (gd, dsum_hbm), (book.at[home, :, D : 2 * D], dx_hbm), (ag, tot_hbm)])
     ]
     outs[0].start()
     outs[1].start()
@@ -387,10 +395,7 @@
 
     outs[2].start()
     exchanged(ag_send, ag_recv).wait_recv()
-    tot_up[0 : D // 2, :] = ag[0 : D // 2, 0:RANK]
-    tot_up[D // 2 : D, :] = ag[0 : D // 2, RANK : 2 * RANK]
-    tot_down[0 : FF // 2, :] = ag[D // 2 : PACKED, 0:RANK]
-    tot_down[FF // 2 : FF, :] = ag[D // 2 : PACKED, RANK : 2 * RANK]
+    outs[3].start()
     exchanged(rs_send, rs_recv).wait_send()
     exchanged(ag_send, ag_recv).wait_send()
     for copy in outs:
@@ -401,15 +406,15 @@
 
 
 def update_kernel(
-    tot_up_hbm, tot_down_hbm, su_hbm, sd_hbm, usum, dsum, dx_in,
+    tot_hbm, su_hbm, sd_hbm, usum, dsum, dx_in,
     new_up, new_down, up_part, down_part, dx_out,
-    tot_up, tot_down, su, sd, nu, nd, dx, pu, pd, in_sem, out_sem,
+    tot, tot_up, tot_down, su, sd, nu, nd, dx, pu, pd, in_sem, out_sem,
 ):
     me = lax.axis_index("dp")
     ub = D // CHUNKS
     db = FF // CHUNKS
     rb = ROWS // CHUNKS
-    small = [(tot_up_hbm, tot_up), (tot_down_hbm, tot_down), (su_hbm, su), (sd_hbm, sd)]
+    small = [(tot_hbm, tot), (su_hbm, su), (sd_hbm, sd)]
     triples = []
     for chunk in range(CHUNKS):
         triples.append((usum, nu, new_up, pl.ds(chunk * ub, ub)))
@@ -434,6 +439,10 @@
         copy.wait()
     ssu = (su[...] * (1.0 / REPLICAS)).astype(BF)
     ssd = (sd[...] * (1.0 / REPLICAS)).astype(BF)
+    tot_up[0 : D // 2, :] = tot[0 : D // 2, 0:RANK]
+    tot_up[D // 2 : D, :] = tot[0 : D // 2, RANK : 2 * RANK]
+    tot_down[0 : FF // 2, :] = tot[D // 2 : PACKED, 0:RANK]
+    tot_down[FF // 2 : FF, :] = tot[D // 2 : PACKED, RANK : 2 * RANK]
     up_rows = D // REPLICAS
     down_rows = FF // REPLICAS
     pu[...] = matmul(tot_up[pl.ds(pl.multiple_of(me * up_rows, up_rows), up_rows), :], ssu)
@@ -454,23 +463,21 @@
     stored_inputs, cotangent, up_weight, down_weight, up_buffer, down_buffer, up_sketch, down_sketch
 ):
     any_spec = pl.BlockSpec(memory_space=pl.ANY)
-    vmem = pl.BlockSpec(memory_space=pltpu.VMEM)
     x = stored_inputs.reshape(ROWS, D)
     cot = cotangent.reshape(ROWS, D)
     sketch_up = jnp.swapaxes(up_sketch[0], 0, 1)
     sketch_down = jnp.swapaxes(down_sketch[0], 0, 1)
-    dx, usum, dsum, tot_up, tot_down = pl.pallas_call(
+    dx, usum, dsum, totals = pl.pallas_call(
         relay_kernel,
         name="relay",
         out_shape=(
             jax.ShapeDtypeStruct((ROWS, D), BF),
             jax.ShapeDtypeStruct((D, FF), F32),
             jax.ShapeDtypeStruct((FF, D), F32),
-            jax.ShapeDtypeStruct((D, RANK), BF),
-            jax.ShapeDtypeStruct((FF, RANK), BF),
+            jax.ShapeDtypeStruct((PACKED, 2 * RANK), BF),
         ),
         in_specs=[any_spec] * 8,
-        out_specs=(any_spec, any_spec, any_spec, vmem, vmem),
+        out_specs=(any_spec,) * 4,
         scratch_shapes=[
             pltpu.VMEM((2, ROWS, D), BF),
             pltpu.VMEM((ROWS, D), BF),
@@ -493,7 +500,7 @@
             pltpu.VMEM((REPLICAS * BLOCK, 2 * RANK), BF),
             pltpu.VMEM((PACKED, 2 * RANK), BF),
             pltpu.SemaphoreType.DMA((8,)),
-            pltpu.SemaphoreType.DMA((3,)),
+            pltpu.SemaphoreType.DMA((4,)),
             pltpu.SemaphoreType.DMA((3,)),
             pltpu.SemaphoreType.DMA((3,)),
             pltpu.SemaphoreType.DMA((PIECES,)),
@@ -520,9 +527,10 @@
             jax.ShapeDtypeStruct((FF // REPLICAS, D), F32),
             jax.ShapeDtypeStruct((ROWS, D), BF),
         ),
-        in_specs=[any_spec] * 7,
+        in_specs=[any_spec] * 6,
         out_specs=(any_spec,) * 5,
         scratch_shapes=[
+            pltpu.VMEM((PACKED, 2 * RANK), BF),
             pltpu.VMEM((D, RANK), BF),
             pltpu.VMEM((FF, RANK), BF),
             pltpu.VMEM((RANK, FF), F32),
@@ -536,7 +544,7 @@
             pltpu.SemaphoreType.DMA((3 * CHUNKS + 2,)),
         ],
         compiler_params=pltpu.CompilerParams(vmem_limit_bytes=60 * 2**20),
-    )(tot_up, tot_down, sketch_up, sketch_down, usum, dsum, dx)
+    )(totals, sketch_up, sketch_down, usum, dsum, dx)
     return (
         grads.reshape(1, 2, ROWS // 2, D),
         new_up[None, None],

time: 98.1 us -> 96.8 us (0.987)
  Pallas kernels: 97.4 us -> 96 us
    pallas_call x1, Pallas kernels: 93.1 us -> 91.8 us  [on_device(): pl.pallas_call(relay_kernel, name='relay', out_shape=(jax.ShapeDtypeStruc...]
where the time goes in v5:
time: 96.8 us; the launch traced here: 96.7 us
  Pallas kernels  96 us (99%)
    pallas_call x1, Pallas kernels, on_device(): pl.pallas_call(relay_kernel, name='relay', out_shape=(jax.ShapeDtypeStruc...  91.8 us
    pallas_call x1, Pallas kernels, on_device(): pl.pallas_call(update_kernel, name='update', out_shape=(jax.ShapeDtypeStr...  4.26 us

profile of v5, /device:TPU:24, one launch (start us, length us, event | category | flops | bytes accessed | tf_op | source)
XLA Modules:
  0.0 96.7 jit_solution(10919169839171206928)
XLA Ops:
  0.6 91.8 %relay.1 = (bf16[1024,512]{1,0:T(8,128)(2,1)}, f32[512,1024]{1,0:T(8,128)}, f32[1024,512]{1,0:T(8,128)}, bf16[768,128]{1,0:T(8,128)(2,1)}) custom-call(bf16[1024,512]{1,0:T(8,128)(2,1)} %bitcast.19, bf16[1024,512]{1,0:T(8,128)(2,1)} %bitcast.20, bf16[512,1024]{1,0:T(8,128)(2,1)} %bitcast.21, bf16[1024,512]{1,0:T(8,128)(2,1)} %bitcast.22, ...), custom_call_target="tpu_custom_call" | custom-call | tf_op jit(solution)/shard_map/relay/pallas_call | solution.py:470
  92.4 4.3 %update.1 = (f32[512,1024]{1,0:T(8,128)}, f32[1024,512]{1,0:T(8,128)}, f32[32,1024]{1,0:T(8,128)}, f32[64,512]{1,0:T(8,128)}, bf16[1024,512]{1,0:T(8,128)(2,1)}) custom-call(bf16[768,128]{1,0:T(8,128)(2,1)} %get-tuple-element.14.tot_hbm, f32[64,1024]{1,0:T(8,128)} %bitcast.24, f32[64,512]{1,0:T(8,128)} %bitcast.26, f32[512,1024]{1,0:T(8,128)} %get-tuple-element.15.usum, ...), custom_call_target="tpu_custom_call" | custom-call | tf_op jit(solution)/shard_map/update/pallas_call | solution.py:520

commit v6 on v5

--- a/solution.py
+++ b/solution.py
@@ -98,16 +98,6 @@
         remote(src, dst, give_send.at[k], give_recv.at[k], (partner, me))
         for k, (src, dst) in enumerate([(wu_hbm, wu.at[1]), (x_hbm, x.at[1]), (wd_hbm, wd.at[1])])
     ]
-    for copy in loads[:3]:
-        copy.start()
-
-    @pl.when(takes_cot)
-    def _():
-        cot_load.start()
-
-    for copy in loads[3:]:
-        copy.start()
-
     barrier = pltpu.get_barrier_semaphore()
 
     me_z = me // DP_Y
@@ -115,18 +105,30 @@
     row = [DP_Y * me_z + lax.rem(me_y + dy, DP_Y) for dy in range(1, DP_Y)]
     column = [DP_Y * lax.rem(me_z + dz, DP_Z) + me_y for dz in range(1, DP_Z)]
 
+    for peer in column:
+        pl.semaphore_signal(barrier, inc=1, device_id=(pos, peer), device_id_type=MESH)
+
+    @pl.when(sends_hop)
+    def _():
+        pl.semaphore_signal(barrier, inc=1, device_id=(target, me), device_id_type=MESH)
+
+    @pl.when(takes_hop)
+    def _():
+        pl.semaphore_signal(barrier, inc=1, device_id=(source, me), device_id_type=MESH)
+
+    for peer in row:
+        pl.semaphore_signal(barrier, inc=1, device_id=(pos, peer), device_id_type=MESH)
     pl.semaphore_signal(barrier, inc=1, device_id=(partner, me), device_id_type=MESH)
 
-    @pl.when(sends_hop)
-    def _():
-        pl.semaphore_signal(barrier, inc=1, device_id=(target, me), device_id_type=MESH)
-
-    @pl.when(takes_hop)
-    def _():
-        pl.semaphore_signal(barrier, inc=1, device_id=(source, me), device_id_type=MESH)
-
-    for peer in row + column:
-        pl.semaphore_signal(barrier, inc=1, device_id=(pos, peer), device_id_type=MESH)
+    for copy in loads[:3]:
+        copy.start()
+
+    @pl.when(takes_cot)
+    def _():
+        cot_load.start()
+
+    for copy in loads[3:]:
+        copy.start()
 
     def span(index, size):
         return pl.ds(pl.multiple_of(index * size, size), size)

time: 96.8 us -> 96.8 us (level)
  no operation moved by 1% of the time
where the time goes in v6:
time: 96.8 us; the launch traced here: 96.7 us
  Pallas kernels  96.1 us (99%)
    pallas_call x1, Pallas kernels, on_device(): pl.pallas_call(relay_kernel, name='relay', out_shape=(jax.ShapeDtypeStruc...  91.8 us
    pallas_call x1, Pallas kernels, on_device(): pl.pallas_call(update_kernel, name='update', out_shape=(jax.ShapeDtypeStr...  4.25 us

profile of v6, /device:TPU:24, one launch (start us, length us, event | category | flops | bytes accessed | tf_op | source)
XLA Modules:
  0.0 96.7 jit_solution(8399594986276745304)
XLA Ops:
  0.6 91.8 %relay.1 = (bf16[1024,512]{1,0:T(8,128)(2,1)}, f32[512,1024]{1,0:T(8,128)}, f32[1024,512]{1,0:T(8,128)}, bf16[768,128]{1,0:T(8,128)(2,1)}) custom-call(bf16[1024,512]{1,0:T(8,128)(2,1)} %bitcast.19, bf16[1024,512]{1,0:T(8,128)(2,1)} %bitcast.20, bf16[512,1024]{1,0:T(8,128)(2,1)} %bitcast.21, bf16[1024,512]{1,0:T(8,128)(2,1)} %bitcast.22, ...), custom_call_target="tpu_custom_call" | custom-call | tf_op jit(solution)/shard_map/relay/pallas_call | solution.py:472
  92.5 4.3 %update.1 = (f32[512,1024]{1,0:T(8,128)}, f32[1024,512]{1,0:T(8,128)}, f32[32,1024]{1,0:T(8,128)}, f32[64,512]{1,0:T(8,128)}, bf16[1024,512]{1,0:T(8,128)(2,1)}) custom-call(bf16[768,128]{1,0:T(8,128)(2,1)} %get-tuple-element.14.tot_hbm, f32[64,1024]{1,0:T(8,128)} %bitcast.24, f32[64,512]{1,0:T(8,128)} %bitcast.26, f32[512,1024]{1,0:T(8,128)} %get-tuple-element.15.usum, ...), custom_call_target="tpu_custom_call" | custom-call | tf_op jit(solution)/shard_map/update/pallas_call | solution.py:522

commit v7 on v5

--- a/solution.py
+++ b/solution.py
@@ -413,14 +413,12 @@
     me = lax.axis_index("dp")
     ub = D // CHUNKS
     db = FF // CHUNKS
-    rb = ROWS // CHUNKS
     small = [(tot_hbm, tot), (su_hbm, su), (sd_hbm, sd)]
     triples = []
     for chunk in range(CHUNKS):
         triples.append((usum, nu, new_up, pl.ds(chunk * ub, ub)))
         triples.append((dsum, nd, new_down, pl.ds(chunk * db, db)))
-    for chunk in range(CHUNKS):
-        triples.append((dx_in, dx, dx_out, pl.ds(chunk * rb, rb)))
+    triples.append((dx_in, dx, dx_out, pl.ds(0, ROWS)))
     count = len(triples)
     early = [pltpu.make_async_copy(src, dst, in_sem.at[count + k]) for k, (src, dst) in enumerate(small)]
     fetch = [
@@ -443,18 +441,18 @@
     tot_up[D // 2 : D, :] = tot[0 : D // 2, RANK : 2 * RANK]
     tot_down[0 : FF // 2, :] = tot[D // 2 : PACKED, 0:RANK]
     tot_down[FF // 2 : FF, :] = tot[D // 2 : PACKED, RANK : 2 * RANK]
+    for k, (src, buf, _, rows) in enumerate(triples):
+        fetch[k].wait()
+        if k < 2 * CHUNKS:
+            total, sketch = (tot_up, ssu) if k % 2 == 0 else (tot_down, ssd)
+            buf[rows, :] = buf[rows, :] - matmul(total[rows, :], sketch)
+        store[k].start()
     up_rows = D // REPLICAS
     down_rows = FF // REPLICAS
     pu[...] = matmul(tot_up[pl.ds(pl.multiple_of(me * up_rows, up_rows), up_rows), :], ssu)
     pd[...] = matmul(tot_down[pl.ds(pl.multiple_of(me * down_rows, down_rows), down_rows), :], ssd)
     store[count].start()
     store[count + 1].start()
-    for k, (src, buf, _, rows) in enumerate(triples):
-        fetch[k].wait()
-        if k < 2 * CHUNKS:
-            total, sketch = (tot_up, ssu) if k % 2 == 0 else (tot_down, ssd)
-            buf[rows, :] = buf[rows, :] - matmul(total[rows, :], sketch)
-        store[k].start()
     for copy in store:
         copy.wait()
 

time: 96.8 us -> 96.8 us (level)
  no operation moved by 1% of the time
where the time goes in v7:
time: 96.8 us; the launch traced here: 96.7 us
  Pallas kernels  96.1 us (99%)
    pallas_call x1, Pallas kernels, on_device(): pl.pallas_call(relay_kernel, name='relay', out_shape=(jax.ShapeDtypeStruc...  91.8 us
    pallas_call x1, Pallas kernels, on_device(): pl.pallas_call(update_kernel, name='update', out_shape=(jax.ShapeDtypeStr...  4.3 us

profile of v7, /device:TPU:24, one launch (start us, length us, event | category | flops | bytes accessed | tf_op | source)
XLA Modules:
  0.0 96.7 jit_solution(6815995900845576382)
XLA Ops:
  0.6 91.8 %relay.1 = (bf16[1024,512]{1,0:T(8,128)(2,1)}, f32[512,1024]{1,0:T(8,128)}, f32[1024,512]{1,0:T(8,128)}, bf16[768,128]{1,0:T(8,128)(2,1)}) custom-call(bf16[1024,512]{1,0:T(8,128)(2,1)} %bitcast.19, bf16[1024,512]{1,0:T(8,128)(2,1)} %bitcast.20, bf16[512,1024]{1,0:T(8,128)(2,1)} %bitcast.21, bf16[1024,512]{1,0:T(8,128)(2,1)} %bitcast.22, ...), custom_call_target="tpu_custom_call" | custom-call | tf_op jit(solution)/shard_map/relay/pallas_call | solution.py:468
  92.4 4.3 %update.1 = (f32[512,1024]{1,0:T(8,128)}, f32[1024,512]{1,0:T(8,128)}, f32[32,1024]{1,0:T(8,128)}, f32[64,512]{1,0:T(8,128)}, bf16[1024,512]{1,0:T(8,128)(2,1)}) custom-call(bf16[768,128]{1,0:T(8,128)(2,1)} %get-tuple-element.14.tot_hbm, f32[64,1024]{1,0:T(8,128)} %bitcast.24, f32[64,512]{1,0:T(8,128)} %bitcast.26, f32[512,1024]{1,0:T(8,128)} %get-tuple-element.15.usum, ...), custom_call_target="tpu_custom_call" | custom-call | tf_op jit(solution)/shard_map/update/pallas_call | solution.py:518
